TPU v7x, 32 devices: a whole 2x2x4 slice. The times are simulated.
32 devices in a mesh: grp: 2 (over x), row: 16 (over z, y, core).
Axes of the slice: x: 2, y: 2, z: 4, core: 2. Of those that a mesh axis runs over, the one named last changes fastest.
Arguments:
- sequence_features: bfloat16 [256, 128, 64], P('grp', 'row'), parts along dimension 0, may hold values from -6 to 6
- edge_features: bfloat16 [256, 128, 128], P(('grp', 'row')), parts along dimension 0, may hold values from -6 to 6
- residue_features: bfloat16 [256, 384], P(('grp', 'row')), parts along dimension 0, may hold values from -6 to 6
- polymer_labels: int32 [256], P('grp'), parts along dimension 0, may hold values from 0 to 7, never falling along the last dimension, each value on 1 to 64 neighbouring positions
- polymer_membership: int32 [16, 128], P('grp'), parts along dimension 0, may hold values from 0 to 1, as said below
- present_residue_flags: int32 [256], P('grp'), parts along dimension 0, may hold values 0 or 1
- sequence_scaling_vector: float32 [64], replicated, may hold values from 0.1 to 1.9
- first_embedding_matrix: bfloat16 [64, 32], replicated, may hold values from -0.75 to 0.75
- second_embedding_matrix: bfloat16 [64, 32], replicated, may hold values from -0.75 to 0.75
- contraction_matrix: bfloat16 [1024, 128], replicated, may hold values from -0.375 to 0.375
- contraction_offset: float32 [128], replicated, may hold values from -3 to 3
- feedforward_scaling_vector: float32 [128], replicated, may hold values from 0.1 to 1.9
- feedforward_switch_matrix: bfloat16 [128, 512], replicated, may hold values from -0.5 to 0.5
- widening_matrix: bfloat16 [128, 512], replicated, may hold values from -0.5 to 0.5
- narrowing_matrix: bfloat16 [512, 128], replicated, may hold values from -0.25 to 0.25
- logit_scaling_vector: float32 [128], replicated, may hold values from 0.1 to 1.9
- edge_logit_matrix: bfloat16 [128, 16], replicated, may hold values from -2 to 2
- residue_scaling_vector: float32 [384], replicated, may hold values from 0.1 to 1.9
- asking_matrix: bfloat16 [384, 384], replicated, as said below
- lookup_matrix: bfloat16 [384, 384], replicated, as said below
- content_matrix: bfloat16 [384, 384], replicated, may hold values from -0.3125 to 0.3125
- heads_sigmoid_matrix: bfloat16 [384, 384], replicated, may hold values from -0.3125 to 0.3125
- heads_merge_matrix: bfloat16 [384, 384], replicated, may hold values from -0.3125 to 0.3125
Outputs:
- pair_out: bfloat16 [256, 128, 128], P(('grp', 'row')), parts along dimension 0
- single_out: bfloat16 [256, 384], P(('grp', 'row')), parts along dimension 0
There are 2 independent parts, one for each index of `grp`. A program takes and returns all parts, laid end to end along the dimension named above; an argument that names none is the same for every part. Nothing has to cross between parts.
Inputs may be any that keep to these rules, and one draw needn't show every extreme that they name: `polymer_labels`: never falling along the tokens. `polymer_membership`: entry [c, s] is 1 where chain c takes part in MSA row s; every chain takes part in exactly 64 rows. `present_residue_flags`: 1 marks a real token. `asking_matrix`: a real matrix. `lookup_matrix`: a real matrix.
All inputs are finite; a program needn't handle non-finite values.
Results may differ from a plain program's by a relative error of at most 0.012.
Values may be sent and summed in bfloat16 or wider, within the bound.
A program may use at most 128 MiB of HBM per device.

v0:
```python
import math

import jax
import jax.numpy as jnp
from jax import lax
from jax.sharding import PartitionSpec as P

epsilon = 1e-05
highest = lax.Precision.HIGHEST


def standardize_features(values, scales):
    values = values.astype(jnp.float32)
    centred = values - jnp.mean(values, axis=-1, keepdims=True)
    spread = jnp.mean(centred * centred, axis=-1, keepdims=True)
    return centred * lax.rsqrt(spread + epsilon) * scales


def local(
    sequence_features,
    edge_features,
    residue_features,
    polymer_labels,
    polymer_membership,
    present_residue_flags,
    sequence_scaling_vector,
    first_embedding_matrix,
    second_embedding_matrix,
    contraction_matrix,
    contraction_offset,
    feedforward_scaling_vector,
    feedforward_switch_matrix,
    widening_matrix,
    narrowing_matrix,
    logit_scaling_vector,
    edge_logit_matrix,
    residue_scaling_vector,
    asking_matrix,
    lookup_matrix,
    content_matrix,
    heads_sigmoid_matrix,
    heads_merge_matrix,
):
    token_row_count = residue_features.shape[0]
    sequence_entries = sequence_features.shape[0]
    sequence_depth = sequence_features.shape[2]
    factor_channels_width = first_embedding_matrix.shape[1]
    pair_width = edge_features.shape[2]
    all_tokens = edge_features.shape[1]
    chains = polymer_membership.shape[0]
    heads = edge_logit_matrix.shape[1]
    single_width = residue_features.shape[1]
    head_size = single_width // heads
    first_token = lax.axis_index("row") * token_row_count
    onehot_all = (polymer_labels[:, None] == jnp.arange(chains, dtype=jnp.int32)[None, :]).astype(
        jnp.float32
    )
    onehot_mine = lax.dynamic_slice_in_dim(onehot_all, first_token, token_row_count, 0)
    pair_rows = polymer_membership.astype(jnp.float32)
    sequence_present_flags = jnp.dot(onehot_mine, pair_rows, precision=highest).T
    shared = jnp.dot(pair_rows, pair_rows.T, precision=highest)
    counts = jnp.dot(
        jnp.dot(onehot_mine, shared, precision=highest), onehot_all.T, precision=highest
    )
    standardized_sequences = standardize_features(
        sequence_features, sequence_scaling_vector
    ).astype(jnp.bfloat16)
    flattened_alignment = standardized_sequences.reshape(
        sequence_entries * token_row_count, sequence_depth
    )
    first_embedding_entries = (
        jnp.dot(
            flattened_alignment, first_embedding_matrix, preferred_element_type=jnp.float32
        ).reshape(sequence_entries, token_row_count, factor_channels_width)
        * sequence_present_flags[:, :, None]
    ).astype(jnp.bfloat16)
    left_flattened = first_embedding_entries.reshape(
        sequence_entries, token_row_count * factor_channels_width
    )
    second_embedding_entries = (
        jnp.dot(
            flattened_alignment, second_embedding_matrix, preferred_element_type=jnp.float32
        ).reshape(sequence_entries, token_row_count, factor_channels_width)
        * sequence_present_flags[:, :, None]
    ).astype(jnp.bfloat16)

    def finish_block(outer, column_start, stride_columns):
        shared_cols = lax.dynamic_slice_in_dim(counts, column_start, stride_columns, 1)
        outer = (outer / jnp.maximum(shared_cols, 1.0)[:, :, None]).astype(jnp.bfloat16)
        update = (
            jnp.dot(
                outer.reshape(
                    token_row_count * stride_columns, factor_channels_width * factor_channels_width
                ),
                contraction_matrix,
                preferred_element_type=jnp.float32,
            )
            + contraction_offset
        )
        old_cols = lax.dynamic_slice_in_dim(edge_features, column_start, stride_columns, 1).reshape(
            token_row_count * stride_columns, pair_width
        )
        return (
            (old_cols.astype(jnp.float32) + update)
            .astype(jnp.bfloat16)
            .reshape(token_row_count, stride_columns, pair_width)
        )

    factor_piece = lax.all_gather(second_embedding_entries, "row", axis=1, tiled=True)
    width = factor_piece.shape[1]
    stride_columns = math.gcd(width, 128)

    def one_block(offset):
        panel = lax.dynamic_slice_in_dim(factor_piece, offset, stride_columns, 1).reshape(
            sequence_entries, stride_columns * factor_channels_width
        )
        outer = lax.dot_general(
            left_flattened, panel, (((0,), (0,)), ((), ())), preferred_element_type=jnp.float32
        )
        outer = outer.reshape(
            token_row_count, factor_channels_width, stride_columns, factor_channels_width
        ).transpose(0, 2, 1, 3)
        outer = outer.reshape(
            token_row_count, stride_columns, factor_channels_width * factor_channels_width
        )
        return finish_block(outer, offset, stride_columns)

    blocks = lax.map(one_block, jnp.arange(0, width, stride_columns, dtype=jnp.int32))
    pair_one = blocks.transpose(1, 0, 2, 3).reshape(token_row_count, width, pair_width)
    flat_pair = pair_one.reshape(token_row_count * all_tokens, pair_width)
    normed_pair = standardize_features(flat_pair, feedforward_scaling_vector).astype(jnp.bfloat16)
    gated = jnp.dot(normed_pair, feedforward_switch_matrix, preferred_element_type=jnp.float32)
    lifted = jnp.dot(normed_pair, widening_matrix, preferred_element_type=jnp.float32)
    hidden = (jax.nn.silu(gated) * lifted).astype(jnp.bfloat16)
    pair_two = (
        flat_pair.astype(jnp.float32)
        + jnp.dot(hidden, narrowing_matrix, preferred_element_type=jnp.float32)
    ).astype(jnp.bfloat16)
    bias_normed = standardize_features(pair_two, logit_scaling_vector).astype(jnp.bfloat16)
    bias_rows = jnp.dot(bias_normed, edge_logit_matrix, preferred_element_type=jnp.float32)
    bias_heads = bias_rows.reshape(token_row_count, all_tokens, heads).transpose(2, 0, 1)
    pair_out = pair_two.reshape(token_row_count, all_tokens, pair_width)
    normed_single = standardize_features(residue_features, residue_scaling_vector).astype(
        jnp.bfloat16
    )
    query = jnp.dot(normed_single, asking_matrix, preferred_element_type=jnp.float32).astype(
        jnp.bfloat16
    )
    query_heads = query.reshape(token_row_count, heads, head_size)
    sigmoid_gate = jax.nn.sigmoid(
        jnp.dot(normed_single, heads_sigmoid_matrix, preferred_element_type=jnp.float32)
    )
    scale = 1.0 / math.sqrt(head_size)
    piece = lax.all_gather(normed_single, "row", axis=0, tiled=True)
    keys_piece = jnp.dot(piece, lookup_matrix, preferred_element_type=jnp.float32).astype(
        jnp.bfloat16
    )
    values_piece = jnp.dot(piece, content_matrix, preferred_element_type=jnp.float32).astype(
        jnp.bfloat16
    )
    width = keys_piece.shape[0]
    key_heads = keys_piece.reshape(width, heads, head_size)
    value_heads = values_piece.reshape(width, heads, head_size)
    scores = (
        jnp.einsum("ihd,jhd->hij", query_heads, key_heads, preferred_element_type=jnp.float32)
        * scale
    )
    scores = scores + bias_heads
    live = (present_residue_flags == 1)[None, None, :]
    scores = jnp.where(live, scores, -1e30)
    peak_old = jnp.full((heads, token_row_count), -1e30, jnp.float32)
    peak_new = jnp.maximum(peak_old, jnp.max(scores, axis=-1))
    expos = jnp.where(live, jnp.exp(scores - peak_new[:, :, None]), 0.0)
    total_new = jnp.sum(expos, axis=-1)
    accum_new = jnp.einsum(
        "hij,jhd->hid", expos.astype(jnp.bfloat16), value_heads, preferred_element_type=jnp.float32
    )
    mixed = accum_new / total_new[:, :, None]
    mixed = mixed.transpose(1, 0, 2).reshape(token_row_count, single_width)
    attended = (mixed * sigmoid_gate).astype(jnp.bfloat16)
    single_out = (
        residue_features.astype(jnp.float32)
        + jnp.dot(attended, heads_merge_matrix, preferred_element_type=jnp.float32)
    ).astype(jnp.bfloat16)
    return (pair_out, single_out)


def solution(mesh):
    placed = (
        P("grp", "row", None),
        P(("grp", "row"), None, None),
        P(("grp", "row"), None),
        P("grp"),
        P("grp", None),
        P("grp"),
        P(),
        P(),
        P(),
        P(),
        P(),
        P(),
        P(),
        P(),
        P(),
        P(),
        P(),
        P(),
        P(),
        P(),
        P(),
        P(),
        P(),
    )
    return jax.shard_map(
        local,
        mesh=mesh,
        in_specs=placed,
        out_specs=(P(("grp", "row"), None, None), P(("grp", "row"), None)),
        check_vma=False,
    )
```

profile of v0, /device:TPU:1, one launch (start us, length us, event | category | flops | bytes accessed | tf_op | source)
XLA Modules:
  0.0 77.3 jit_solution(2994039761496273403)
XLA Ops:
  7.2 0.0 copy-start
  7.2 0.0 copy-start.1
  7.2 0.0 copy-start.5
  7.2 0.0 copy-start.8
  7.2 0.0 all-gather.2.cloned.1.call-start
  7.3 0.8 %iota_compare_fusion = pred[128,8]{1,0:T(8,128)(4,1)S(1)} fusion(s32[128]{0:T(128)} %param.26), kind=kLoop, calls=%fused_computation.68 | loop fusion | flops 1024 | bytes 1536 | tf_op jit(solution)/shard_map/eq | solution.py:55
  8.1 0.9 %convert_reduce_fusion.1 = f32[128,8]{0,1:T(8,128)S(1)} fusion(bf16[128,8,64]{0,2,1:T(8,128)(2,1)} %param.23), kind=kLoop, calls=%fused_computation.50 | loop fusion | flops 130048 | bytes 135168 | tf_op jit(solution)/shard_map/reduce_sum | solution.py:14
  9.1 1.0 %fusion.42 = f32[128,8]{0,1:T(8,128)S(1)} fusion(bf16[128,8,64]{0,2,1:T(8,128)(2,1)} %param.23, f32[128,8]{0,1:T(8,128)S(1)} %broadcast_multiply_fusion.2), kind=kLoop, calls=%fused_computation.54 | loop fusion | flops 261120 | bytes 139264 | tf_op jit(solution)/shard_map/reduce_sum | solution.py:15
  10.1 0.8 %convolution_bitcast_fusion.3 = f32[128,8]{0,1:T(8,128)S(1)} fusion(s32[8,128]{1,0:T(8,128)} %param.27, pred[128,8]{1,0:T(8,128)(4,1)S(1)} %iota_compare_fusion, s32[]{:T(128)S(6)} %select_n.14), kind=kOutput, calls=%fused_computation.34 | convolution fusion | flops 99328 | bytes 9220 | tf_op jit(solution)/shard_map/dot_general | solution.py:60
  10.9 1.8 %fusion.19 = bf16[128,8,32]{0,2,1:T(8,128)(2,1)} fusion(f32[128,8]{0,1:T(8,128)S(1)} %convolution_bitcast_fusion.3, bf16[128,8,64]{0,2,1:T(8,128)(2,1)} %param.23, f32[64]{0:T(128)} %param.29, f32[128,8]{0,1:T(8,128)S(1)} %add_rsqrt_fusion.2, f32[128,8]{0,1:T(8,128)S(1)} %broadcast_multiply_fusion.2, bf16[64,32]{0,1:T(8,128)(2,1)} %param.31), kind=kOutput, calls=%fused_computation.17 | convolution fusion | flops 4587520 | bytes 213248 | tf_op jit(solution)/shard_map/dot_general | solution.py:81
  12.6 0.0 all-gather.2.cloned.1.call-update
  12.7 0.8 %convert_reduce_fusion.2 = f32[8]{0:T(128)S(1)} fusion(bf16[8,384]{1,0:T(8,128)(2,1)} %param.25), kind=kLoop, calls=%fused_computation.76 | loop fusion | flops 6136 | bytes 6176 | tf_op jit(solution)/shard_map/reduce_sum | solution.py:14
  13.5 0.9 %fusion.71 = f32[8]{0:T(128)S(1)} fusion(bf16[8,384]{1,0:T(8,128)(2,1)} %param.25, f32[8]{0:T(128)S(1)} %broadcast_multiply_fusion.3), kind=kLoop, calls=%fused_computation.79 | loop fusion | flops 12280 | bytes 6208 | tf_op jit(solution)/shard_map/reduce_sum | solution.py:15
  14.4 0.8 %fusion.73 = bf16[8,384]{1,0:T(8,128)(2,1)S(1)} fusion(bf16[8,384]{1,0:T(8,128)(2,1)} %param.25, f32[384]{0:T(512)} %param.40, f32[8]{0:T(128)S(1)} %add_rsqrt_fusion.3, f32[8]{0:T(128)S(1)} %broadcast_multiply_fusion.3), kind=kLoop, calls=%fused_computation.81 | loop fusion | flops 15360 | bytes 13888 | tf_op jit(solution)/shard_map/convert_element_type | solution.py:143
  15.1 23.2 %all_gather.7 = bf16[128,384]{1,0:T(8,128)(2,1)S(1)} all-gather(bf16[8,384]{1,0:T(8,128)(2,1)S(1)} %fusion.73), channel_id=1, replica_groups=mesh['grp'=2,'row'=16] {'row'}, dimensions={0}, use_global_device_ids=true | all-gather | bytes 104448 | tf_op jit(solution)/shard_map/all_gather | solution.py:154
  38.4 0.2 convolution_convert_fusion.1
  38.6 0.1 copy.36
  38.7 1.2 %convolution_convert_fusion.2 = bf16[8,384]{1,0:T(8,128)(2,1)S(1)} fusion(bf16[384,384]{1,0:T(8,128)(2,1)} %param.41, bf16[8,384]{1,0:T(8,128)(2,1)} %param.25, f32[384]{0:T(512)} %param.40, f32[8]{0:T(128)S(1)} %add_rsqrt_fusion.3, f32[8]{0:T(128)S(1)} %broadcast_multiply_fusion.3), kind=kOutput, calls=%fused_computation.33 | convolution fusion | flops 2377728 | bytes 308800 | tf_op jit(solution)/shard_map/dot_general | solution.py:146
  39.9 0.1 reshape.122
  40.0 1.2 %convolution_convert_fusion = bf16[128,384]{1,0:T(8,128)(2,1)S(1)} fusion(bf16[128,384]{1,0:T(8,128)(2,1)S(1)} %all_gather.7, bf16[384,384]{1,0:T(8,128)(2,1)} %param.43), kind=kOutput, calls=%fused_computation.12 | convolution fusion | flops 37797888 | bytes 491520 | tf_op jit(solution)/shard_map/dot_general | solution.py:158
  41.2 0.1 copy.38
  41.4 0.1 fusion.78
  41.5 0.1 fusion.81
  41.6 0.0 copy-done.10
  41.6 0.2 fusion.30
  41.8 0.1 broadcast_compare_fusion
  41.9 11.4 %all-gather.2.cloned.1.call-done = bf16[128,128,32]{0,2,1:T(8,128)(2,1)} async-done(((bf16[128,8,32]{0,2,1:T(8,128)(2,1)}), bf16[128,128,32]{0,2,1:T(8,128)(2,1)}) %all-gather.2.cloned.1.call-update) | async-done | bytes 1048592 | tf_op jit(solution)/shard_map/all_gather | solution.py:109
  53.3 0.0 copy-done.1
  53.3 4.0 %convolution_bitcast_fusion = f32[8,128,32,32]{1,2,3,0:T(8,128)} fusion(bf16[128,32,128]{2,1,0:T(8,128)(2,1)} %bitcast.86, f32[128,8]{0,1:T(8,128)S(1)} %convolution_bitcast_fusion.3, bf16[128,8,64]{0,2,1:T(8,128)(2,1)S(1)} %copy-done.1, f32[64]{0:T(128)S(1)} %copy-done.8, f32[128,8]{0,1:T(8,128)S(1)} %add_rsqrt_fusion.2, ...), kind=kOutput, calls=%fused_computation.2 | convolution fusion | flops 273022976 | bytes 5390592 | tf_op jit(solution)/shard_map/while/body/eval_jaxpr/dot_general | solution.py:117
  57.3 4.7 %copy.35 = f32[8,128,32,32]{1,0,3,2:T(8,128)S(1)} copy(f32[8,128,32,32]{1,2,3,0:T(8,128)} %convolution_bitcast_fusion) | data formatting | bytes 8388608 | tf_op jit(solution)/shard_map/while/body/eval_jaxpr/transpose | solution.py:122
  62.0 0.0 copy-start.3
  62.0 0.0 copy-start.9
  62.0 1.3 %fusion.92 = (f32[1024]{0:T(1024)S(1)}, f32[1024,128]{1,0:T(8,128)S(1)}) fusion(f32[128]{0:T(128)S(1)} %copy-done.15, bf16[1024,128]{1,0:T(8,128)(2,1)S(1)} %copy-done.11, f32[128,8,8,128]{3,2,1,0:T(8,128)S(1)} %bitcast.85, f32[1024]{0:T(1024)S(1)} %fusion.30, bf16[1024,128]{1,0:T(8,128)(2,1)S(1)} %bitcast.92), kind=kOutput, calls=%fused_computation.106 | convolution fusion | flops 271318016 | bytes 5251584 | tf_op jit(solution)/shard_map/while/body/eval_jaxpr/dot_general | solution.py:91
  63.3 0.4 multiply_reduce_fusion
  63.7 0.5 fusion.41
  64.2 0.0 copy-start.13
  64.2 0.0 copy-start.16
  64.2 0.0 copy-start.4
  64.2 0.0 copy-start.7
  64.3 2.0 %convert_reduce_fusion = (f32[1024]{0:T(1024)S(1)}, bf16[1024,128]{1,0:T(8,128)(2,1)S(1)}) fusion(f32[1024,128]{1,0:T(8,128)S(1)} %get-tuple-element.19, bf16[512,128]{1,0:T(8,128)(2,1)} %param.37, f32[1024,512]{1,0:T(8,128)S(1)} %fusion.41, bf16[128,512]{1,0:T(8,128)(2,1)} %param.35, f32[128]{0:T(128)S(1)} %copy-done.9, f32[1024]{0:T(1024)S(1)} %add_rsqrt_fusion.1, ...), kind=kOutput, calls=%fused_computation.41 | convolution fusion | flops 272628736 | bytes 3158528 | tf_op jit(solution)/shard_map/dot_general | solution.py:137
  66.3 0.0 copy-start.2
  66.3 0.4 fusion.36
  66.7 0.9 %convolution_bitcast_fusion.2 = f32[2,8,8,128]{3,1,2,0:T(8,128)S(1)} fusion(bf16[128,16]{0,1:T(8,128)(2,1)S(1)} %copy-done.13, bf16[1024,128]{1,0:T(8,128)(2,1)S(1)} %get-tuple-element.21, f32[128]{0:T(128)S(1)} %copy-done.16, f32[1024]{0:T(1024)S(1)} %add_rsqrt_fusion, f32[1024]{0:T(1024)S(1)} %broadcast_multiply_fusion), kind=kOutput, calls=%fused_computation.21 | convolution fusion | flops 4849664 | bytes 340480 | tf_op jit(solution)/shard_map/dot_general | solution.py:140
  67.7 0.2 fusion.93
  67.9 0.2 fusion.59
  68.1 0.2 fusion.21
  68.3 0.1 reshape.126
  68.5 2.0 %fusion.29 = bf16[8,384]{1,0:T(8,128)(2,1)} fusion(bf16[384,384]{1,0:T(8,128)(2,1)} %param.45, f32[8,384]{1,0:T(8,128)S(1)} %reshape.126, bf16[384,384]{1,0:T(8,128)(2,1)} %param.44, bf16[8,384]{1,0:T(8,128)(2,1)S(1)} %copy-done.4, f32[384]{0:T(512)S(1)} %copy-done.7, f32[8]{0:T(128)S(1)} %add_rsqrt_fusion.3, f32[8]{0:T(128)S(1)} %broadcast_multiply_fusion.3), kind=kOutput, calls=%fused_computation.32 | convolution fusion | flops 4758528 | bytes 616000 | tf_op jit(solution)/shard_map/dot_general | solution.py:183
  (32 shorter events, 0.1 us)
Async XLA Ops:
  7.2 31.2 %copy-start = (bf16[384,384]{1,0:T(8,128)(2,1)S(1)}, bf16[384,384]{1,0:T(8,128)(2,1)}, u32[]{:S(2)}) copy-start(bf16[384,384]{1,0:T(8,128)(2,1)} %param.42) | copy-start | bytes 884740
  7.2 34.4 %copy-start.10 = (s32[128]{0:T(128)S(1)}, s32[128]{0:T(128)}, u32[]{:S(2)}) copy-start(s32[128]{0:T(128)} %param.26) | copy-start | bytes 1540
  7.2 46.1 %copy-start.1 = (bf16[128,8,64]{0,2,1:T(8,128)(2,1)S(1)}, bf16[128,8,64]{0,2,1:T(8,128)(2,1)}, u32[]{:S(2)}) copy-start(bf16[128,8,64]{0,2,1:T(8,128)(2,1)} %param.23) | copy-start | bytes 393220
  7.2 34.1 %copy-start.5 = (s32[8,128]{1,0:T(8,128)S(1)}, s32[8,128]{1,0:T(8,128)}, u32[]{:S(2)}) copy-start(s32[8,128]{1,0:T(8,128)} %param.27) | copy-start | bytes 12292
  7.2 46.1 %copy-start.8 = (f32[64]{0:T(128)S(1)}, f32[64]{0:T(128)}, u32[]{:S(2)}) copy-start(f32[64]{0:T(128)} %param.29) | copy-start | bytes 772
  7.2 34.6 %copy-start.14 = (s32[128]{0:T(128)S(1)}, s32[128]{0:T(128)}, u32[]{:S(2)}) copy-start(s32[128]{0:T(128)} %param.28) | copy-start | bytes 1540
  7.2 46.0 %copy-start.6 = (bf16[64,32]{0,1:T(8,128)(2,1)S(1)}, bf16[64,32]{0,1:T(8,128)(2,1)}, u32[]{:S(2)}) copy-start(bf16[64,32]{0,1:T(8,128)(2,1)} %param.30) | copy-start | bytes 12292
  7.2 46.0 %all-gather.2.cloned.1.call-start = ((), (), s32[]{:S(2)}) async-start(), calls=%async_computation | async-start | bytes 1114112 | tf_op jit(solution)/shard_map/all_gather | solution.py:109
  57.3 4.7 %copy-start.11 = (bf16[1024,128]{1,0:T(8,128)(2,1)S(1)}, bf16[1024,128]{1,0:T(8,128)(2,1)}, u32[]{:S(2)}) copy-start(bf16[1024,128]{1,0:T(8,128)(2,1)} %param.32) | copy-start | bytes 786436
  57.3 4.7 %copy-start.12 = (bf16[8,128,128]{2,1,0:T(8,128)(2,1)S(1)}, bf16[8,128,128]{2,1,0:T(8,128)(2,1)}, u32[]{:S(2)}) copy-start(bf16[8,128,128]{2,1,0:T(8,128)(2,1)} %param.24) | copy-start | bytes 786436
  57.3 4.7 %copy-start.15 = (f32[128]{0:T(128)S(1)}, f32[128]{0:T(128)}, u32[]{:S(2)}) copy-start(f32[128]{0:T(128)} %param.33) | copy-start | bytes 1540
  62.0 1.7 %copy-start.3 = (bf16[128,512]{1,0:T(8,128)(2,1)S(1)}, bf16[128,512]{1,0:T(8,128)(2,1)}, u32[]{:S(2)}) copy-start(bf16[128,512]{1,0:T(8,128)(2,1)} %param.36) | copy-start | bytes 393220
  62.0 1.7 %copy-start.9 = (f32[128]{0:T(128)S(1)}, f32[128]{0:T(128)}, u32[]{:S(2)}) copy-start(f32[128]{0:T(128)} %param.34) | copy-start | bytes 1540
  64.2 2.5 %copy-start.13 = (bf16[128,16]{0,1:T(8,128)(2,1)S(1)}, bf16[128,16]{0,1:T(8,128)(2,1)}, u32[]{:S(2)}) copy-start(bf16[128,16]{0,1:T(8,128)(2,1)} %param.39) | copy-start | bytes 12292
  64.2 2.5 %copy-start.16 = (f32[128]{0:T(128)S(1)}, f32[128]{0:T(128)}, u32[]{:S(2)}) copy-start(f32[128]{0:T(128)} %param.38) | copy-start | bytes 1540
  64.2 4.2 %copy-start.4 = (bf16[8,384]{1,0:T(8,128)(2,1)S(1)}, bf16[8,384]{1,0:T(8,128)(2,1)}, u32[]{:S(2)}) copy-start(bf16[8,384]{1,0:T(8,128)(2,1)} %param.25) | copy-start | bytes 18436
  64.2 4.2 %copy-start.7 = (f32[384]{0:T(512)S(1)}, f32[384]{0:T(512)}, u32[]{:S(2)}) copy-start(f32[384]{0:T(512)} %param.40) | copy-start | bytes 4612
  66.3 4.1 %copy-start.2 = (bf16[1024,128]{1,0:T(8,128)(2,1)}, bf16[1024,128]{1,0:T(8,128)(2,1)S(1)}, u32[]{:S(2)}) copy-start(bf16[1024,128]{1,0:T(8,128)(2,1)S(1)} %get-tuple-element.21) | copy-start | bytes 786436
Sparse Core Ops, SparseCore 0:
  12.8 40.4 all-gather.1
where the time goes:
time: 78 us; the launch traced here: 77.3 us
  blocking collectives  23.2 us (30%)
  matrix products  16.8 us (22%)
  between operations  14.4 us (18%)
  waiting for transfers between devices  11.4 us (15%)
  other arithmetic  6.2 us (8%)
  local copies, waits for them, and re-layouts  5.24 us (7%)
    all_gather x1, blocking collectives, local(): piece = lax.all_gather(normed_single, 'row', axis=0, tiled=True)  23.2 us
    all_gather x1, waiting for transfers between devices, local(): lax.all_gather(second_embedding_entries, 'row', axis=1, tiled=True)  11.4 us
    transpose x1, local copies, waits for them, and re-layouts, one_block(): outer = outer.reshape(token_row_count, factor_channels_width, stride_colu...  4.68 us
    dot_general x1, matrix products, one_block(): lax.dot_general(left_flattened, panel, (((0,), (0,)), ((), ())), preferre...  4.04 us
    reduce_sum x4, other arithmetic, standardize_features(): spread = jnp.mean(centred * centred, axis=-1, keepdims=True)  2.55 us
    dot_general x1, matrix products, local(): jnp.dot(hidden, narrowing_matrix, preferred_element_type=jnp.float32)  2.04 us
    dot_general x1, matrix products, local(): jnp.dot(attended, heads_merge_matrix, preferred_element_type=jnp.float32)  2 us
    dot_general x1, matrix products, local(): jnp.dot(flattened_alignment, second_embedding_matrix, preferred_element_t...  1.76 us
  transfers between devices with their start and end apart: 1, of which 1 were waited for; matrix products, arithmetic and copies ran while one was open for 8% of the time, Pallas kernels for 0%

commit v1 on v0

v1 whole, which is shorter than its diff:
```python
import functools
import math

import jax
import jax.numpy as jnp
from jax import lax
from jax.experimental import pallas as pl
from jax.experimental.pallas import tpu as pltpu
from jax.sharding import PartitionSpec as P

epsilon = 1e-05
highest = lax.Precision.HIGHEST
F32 = jnp.float32
BF16 = jnp.bfloat16


def standardize_features(values, scales):
    values = values.astype(F32)
    centred = values - jnp.mean(values, axis=-1, keepdims=True)
    spread = jnp.mean(centred * centred, axis=-1, keepdims=True)
    return centred * lax.rsqrt(spread + epsilon) * scales


def digits(count):
    core = 2 if count % 2 == 0 else 1
    chips = count // core
    fast = 1
    while chips % (fast * 2) == 0 and (fast * 2) ** 2 <= chips:
        fast *= 2
    return chips // fast, fast, core


def gather_kernel(count, right_in, single_in, right_out, single_out, send_sem, recv_sem):
    slow, fast, core = digits(count)
    me = lax.axis_index("row")
    my_core = lax.rem(me, core)
    chip = lax.div(me, core)
    my_fast = lax.rem(chip, fast)
    my_slow = lax.div(chip, fast)

    def place(a, b, c):
        return (a * fast + b) * core + c

    slow_digits = [lax.rem(my_slow + k, slow) for k in range(slow)]
    fast_digits = [lax.rem(my_fast + k, fast) for k in range(fast)]
    other_core = lax.rem(my_core + 1, core)
    slow_peers = [place(a, my_fast, my_core) for a in slow_digits[1:]]
    fast_peers = [place(my_slow, b, my_core) for b in fast_digits[1:]]
    core_peers = [place(my_slow, my_fast, other_core)] if core == 2 else []
    peers = slow_peers + fast_peers + core_peers

    barrier = pltpu.get_barrier_semaphore()
    for peer in peers:
        pl.semaphore_signal(
            barrier, inc=1, device_id={"row": peer}, device_id_type=pl.DeviceIdType.MESH
        )
    right_out[:, me] = right_in[...]
    single_out[me] = single_in[...]
    pl.semaphore_wait(barrier, len(peers))

    started = []

    def copies(origin, peer, sent, own):
        pair = []
        for which, (entry, result) in enumerate(
            (
                (right_in, right_out.at[:, origin]),
                (single_in, single_out.at[origin]),
            )
        ):
            pair.append(
                pltpu.make_async_remote_copy(
                    src_ref=entry if own else result,
                    dst_ref=result,
                    send_sem=send_sem.at[which, sent],
                    recv_sem=recv_sem.at[which, origin],
                    device_id={"row": peer},
                    device_id_type=pl.DeviceIdType.MESH,
                )
            )
        return pair

    def send(origin, targets, own=False):
        for peer in targets:
            for copy in copies(origin, peer, len(started) // 2, own):
                copy.start()
                started.append(copy)

    def arrive(origin):
        for copy in copies(origin, peers[0], 0, False):
            copy.wait_recv()

    send(me, peers, own=True)
    for a in slow_digits[1:]:
        origin = place(a, my_fast, my_core)
        arrive(origin)
        send(origin, fast_peers + core_peers)
    for b in fast_digits[1:]:
        for a in slow_digits:
            origin = place(a, b, my_core)
            arrive(origin)
            send(origin, core_peers)
    if core == 2:
        for b in fast_digits:
            for a in slow_digits:
                arrive(place(a, b, other_core))
    for copy in started:
        copy.wait_send()


def gather(count, right, single):
    slow, fast, core = digits(count)
    sends = (slow - 1) + slow * (fast - 1) + (slow * fast if core == 2 else 0)
    depth, tokens_here, entries = right.shape
    return pl.pallas_call(
        functools.partial(gather_kernel, count),
        out_shape=(
            jax.ShapeDtypeStruct((depth, count, tokens_here, entries), right.dtype),
            jax.ShapeDtypeStruct((count,) + single.shape, single.dtype),
        ),
        in_specs=[pl.BlockSpec(memory_space=pltpu.VMEM)] * 2,
        out_specs=(pl.BlockSpec(memory_space=pltpu.VMEM),) * 2,
        scratch_shapes=[
            pltpu.SemaphoreType.DMA((2, sends)),
            pltpu.SemaphoreType.DMA((2, count)),
        ],
        compiler_params=pltpu.CompilerParams(
            collective_id=0, has_side_effects=True, vmem_limit_bytes=48 * 2**20
        ),
        name="gather",
    )(right, single)


def dot(a, b):
    return jnp.dot(a, b, preferred_element_type=F32)


def dot_nt(a, b):
    return lax.dot_general(a, b, (((1,), (1,)), ((), ())), preferred_element_type=F32)


def finish_kernel(
    left,
    right,
    counts,
    edge,
    contraction,
    offset,
    ff_scale,
    switch,
    widening,
    narrowing,
    logit_scale,
    edge_logit,
    residue,
    normed_mine,
    normed_all,
    flags,
    asking,
    lookup,
    content,
    gate_matrix,
    merge,
    pair_out,
    single_out,
    total,
    bias,
):
    rows, tokens, width = edge.shape
    entries = right.shape[2]
    pairs = contraction.shape[0]
    heads = edge_logit.shape[0]
    single_width = residue.shape[1]
    head_size = single_width // heads

    total[...] = jnp.zeros_like(total)

    def contract(k, carry):
        mixed = dot(left[...], contraction[k]).astype(BF16)
        columns = []
        for i in range(rows):
            part = mixed[i * entries : (i + 1) * entries]
            columns.append(jnp.concatenate([part[:, :width], part[:, width:]], axis=0))
        panel = jnp.concatenate([right[2 * k], right[2 * k + 1]], axis=1)
        total[...] += dot(panel, jnp.concatenate(columns, axis=1))
        return carry

    lax.fori_loop(0, pairs, contract, 0, unroll=2)

    def transition(i):
        divisor = 1.0 / jnp.maximum(counts[:, i : i + 1], 1.0)
        pair_one = (
            edge[i].astype(F32) + (total[:, i * width : (i + 1) * width] * divisor + offset[...])
        ).astype(BF16)
        normed = standardize_features(pair_one, ff_scale[...]).astype(BF16)
        gated = dot(normed, switch[...])
        lifted = dot(normed, widening[...])
        hidden = (gated / (1.0 + jnp.exp(-gated)) * lifted).astype(BF16)
        pair_two = (pair_one.astype(F32) + dot(hidden, narrowing[...])).astype(BF16)
        pair_out[i] = pair_two
        bias_normed = standardize_features(pair_two, logit_scale[...]).astype(BF16)
        bias[i] = dot_nt(edge_logit[...], bias_normed)

    for i in range(rows):
        transition(i)

    keys = dot(normed_all[...], lookup[...]).astype(BF16)
    values = dot(normed_all[...], content[...]).astype(BF16)
    query = dot(normed_mine[...], asking[...]).astype(BF16).astype(F32)
    gate = jax.nn.sigmoid(dot(normed_mine[...], gate_matrix[...]))
    first = lax.broadcasted_iota(jnp.int32, (heads, single_width), 0) * head_size
    channel = lax.broadcasted_iota(jnp.int32, (heads, single_width), 1)
    mine = ((channel >= first) & (channel < first + head_size)).astype(F32)
    spread = jnp.concatenate([query[i : i + 1] * mine for i in range(rows)], axis=0).astype(BF16)
    scores = dot_nt(spread, keys) * (1.0 / math.sqrt(head_size)) + bias[...].reshape(
        rows * heads, tokens
    )
    live = flags[...] == 1
    scores = jnp.where(live, scores, -1e30)
    peak = jnp.max(scores, axis=-1, keepdims=True)
    expos = jnp.where(live, jnp.exp(scores - peak), 0.0)
    sums = jnp.sum(expos, axis=-1, keepdims=True)
    blended = dot(expos.astype(BF16), values) / sums
    attended = jnp.concatenate(
        [
            jnp.sum(blended[i * heads : (i + 1) * heads] * mine, axis=0, keepdims=True)
            for i in range(rows)
        ],
        axis=0,
    )
    attended = (attended * gate).astype(BF16)
    single_out[...] = (residue[...].astype(F32) + dot(attended, merge[...])).astype(BF16)


def finish(*arrays):
    edge, edge_logit, residue = arrays[3], arrays[11], arrays[12]
    rows, tokens, width = edge.shape
    return pl.pallas_call(
        finish_kernel,
        out_shape=(
            jax.ShapeDtypeStruct(edge.shape, edge.dtype),
            jax.ShapeDtypeStruct(residue.shape, residue.dtype),
        ),
        in_specs=[pl.BlockSpec(memory_space=pltpu.VMEM)] * len(arrays),
        out_specs=(pl.BlockSpec(memory_space=pltpu.VMEM),) * 2,
        scratch_shapes=[
            pltpu.VMEM((tokens, rows * width), F32),
            pltpu.VMEM((rows, edge_logit.shape[0], tokens), F32),
        ],
        compiler_params=pltpu.CompilerParams(vmem_limit_bytes=56 * 2**20),
        name="finish",
    )(*arrays)


def local(
    sequence_features,
    edge_features,
    residue_features,
    polymer_labels,
    polymer_membership,
    present_residue_flags,
    sequence_scaling_vector,
    first_embedding_matrix,
    second_embedding_matrix,
    contraction_matrix,
    contraction_offset,
    feedforward_scaling_vector,
    feedforward_switch_matrix,
    widening_matrix,
    narrowing_matrix,
    logit_scaling_vector,
    edge_logit_matrix,
    residue_scaling_vector,
    asking_matrix,
    lookup_matrix,
    content_matrix,
    heads_sigmoid_matrix,
    heads_merge_matrix,
):
    rows, tokens, width = edge_features.shape
    entries, _, depth = sequence_features.shape
    factors = first_embedding_matrix.shape[1]
    chains = polymer_membership.shape[0]
    single_width = residue_features.shape[1]
    count = lax.axis_size("row")
    first_token = lax.axis_index("row") * rows

    normed_single = standardize_features(residue_features, residue_scaling_vector).astype(BF16)
    onehot_all = (
        polymer_labels[:, None] == jnp.arange(chains, dtype=jnp.int32)[None, :]
    ).astype(F32)
    onehot_mine = lax.dynamic_slice_in_dim(onehot_all, first_token, rows, 0)
    membership = polymer_membership.astype(F32)
    present = jnp.dot(onehot_mine, membership, precision=highest)
    shared = jnp.dot(membership, membership.T, precision=highest)
    counts = jnp.dot(
        jnp.dot(onehot_all, shared, precision=highest), onehot_mine.T, precision=highest
    )

    alignment = standardize_features(
        sequence_features.transpose(1, 0, 2), sequence_scaling_vector
    ).astype(BF16)
    left = (
        lax.dot_general(
            alignment,
            first_embedding_matrix,
            (((2,), (0,)), ((), ())),
            preferred_element_type=F32,
        )
        * present[:, :, None]
    ).astype(BF16)
    right = (
        lax.dot_general(
            second_embedding_matrix,
            alignment,
            (((0,), (2,)), ((), ())),
            preferred_element_type=F32,
        )
        * present[None]
    ).astype(BF16)

    right_all, single_all = gather(count, right, normed_single)
    paired = contraction_matrix.reshape(factors, factors // 2, 2 * width).transpose(1, 0, 2)
    return finish(
        left.reshape(rows * entries, factors),
        right_all.reshape(factors, tokens, entries),
        counts,
        edge_features,
        paired,
        contraction_offset[None],
        feedforward_scaling_vector[None],
        feedforward_switch_matrix,
        widening_matrix,
        narrowing_matrix,
        logit_scaling_vector[None],
        edge_logit_matrix.T,
        residue_features,
        normed_single,
        single_all.reshape(tokens, single_width),
        present_residue_flags[None],
        asking_matrix,
        lookup_matrix,
        content_matrix,
        heads_sigmoid_matrix,
        heads_merge_matrix,
    )


def solution(mesh):
    placed = (
        P("grp", "row", None),
        P(("grp", "row"), None, None),
        P(("grp", "row"), None),
        P("grp"),
        P("grp", None),
        P("grp"),
        P(),
        P(),
        P(),
        P(),
        P(),
        P(),
        P(),
        P(),
        P(),
        P(),
        P(),
        P(),
        P(),
        P(),
        P(),
        P(),
        P(),
    )
    return jax.shard_map(
        local,
        mesh=mesh,
        in_specs=placed,
        out_specs=(P(("grp", "row"), None, None), P(("grp", "row"), None)),
        check_vma=False,
    )
```

time: 78 us -> 46.3 us (0.59)
  Pallas kernels: 0 us -> 33.6 us
  blocking collectives: 23.2 us -> 0 us
  matrix products: 16.8 us -> 2.44 us
  between operations: 14.4 us -> 0.78 us
  waiting for transfers between devices: 11.4 us -> 0 us
  other arithmetic: 6.2 us -> 3.05 us
    pallas_call x0 -> x2, Pallas kernels: none -> 33.6 us  [the longest x1 18.5 us: gather(): pl.pallas_call(functools.partial(gather_kernel, count), out_shape=(jax.Sh...]
    all_gather x1 -> x0, blocking collectives: 23.2 us -> none  [local(): piece = lax.all_gather(normed_single, 'row', axis=0, tiled=True)]
    dot_general x16 -> x6, matrix products: 16.8 us -> 2.44 us  [the longest x1 0.89 us: local(): shared = jnp.dot(membership, membership.T, precision=highest)]
    all_gather x1 -> x0, waiting for transfers between devices: 11.4 us -> none  [local(): lax.all_gather(second_embedding_entries, 'row', axis=1, tiled=True)]
    transpose x1 -> x0, local copies, waits for them, and re-layouts: 4.68 us -> none  [one_block(): outer = outer.reshape(token_row_count, factor_channels_width, stride_colu...]
    unnamed x35 -> x24, local copies, waits for them, and re-layouts: 0.11 us -> 4.05 us
    reduce_sum x4 -> x2, other arithmetic: 2.55 us -> 0.92 us  [standardize_features(): spread = jnp.mean(centred * centred, axis=-1, keepdims=True)]
  transfers between devices with their start and end apart: 1 -> 0, of which waited for: 1 -> 0; matrix products, arithmetic and copies ran while one was open for 8% -> 0% of each run, Pallas kernels for 0% -> 0%
where the time goes in v1:
time: 46.3 us; the launch traced here: 45.7 us
  Pallas kernels  33.6 us (73%)
  local copies, waits for them, and re-layouts  5.79 us (13%)
  other arithmetic  3.05 us (7%)
  matrix products  2.44 us (5%)
  between operations  0.78 us (2%)
    pallas_call x1, Pallas kernels, gather(): pl.pallas_call(functools.partial(gather_kernel, count), out_shape=(jax.Sh...  18.5 us
    pallas_call x1, Pallas kernels, finish(): pl.pallas_call(finish_kernel, out_shape=(jax.ShapeDtypeStruct(edge.shape,...  15.2 us
    unnamed x24, local copies, waits for them, and re-layouts  4.05 us
    reduce_sum x2, other arithmetic, standardize_features(): centred = values - jnp.mean(values, axis=-1, keepdims=True)  1.78 us

profile of v1, /device:TPU:1, one launch (start us, length us, event | category | flops | bytes accessed | tf_op | source)
XLA Modules:
  0.0 45.7 jit_solution(560268912397377461)
XLA Ops:
  0.6 0.0 copy-start
  0.6 0.0 copy-start.4
  0.7 0.8 %convert_reduce_fusion = f32[8]{0:T(128)S(1)} fusion(bf16[8,384]{1,0:T(8,128)(2,1)} %residue.1), kind=kLoop, calls=%fused_computation.17 | loop fusion | flops 6136 | bytes 6176 | tf_op jit(solution)/shard_map/reduce_sum | solution.py:19
  1.5 0.9 %fusion.14 = f32[8]{0:T(128)S(1)} fusion(bf16[8,384]{1,0:T(8,128)(2,1)} %residue.1, f32[8]{0:T(128)S(1)} %broadcast_multiply_fusion.1), kind=kLoop, calls=%fused_computation.20 | loop fusion | flops 12280 | bytes 6208 | tf_op jit(solution)/shard_map/reduce_sum | solution.py:20
  2.4 0.9 %fusion.19 = f32[8,8]{1,0:T(8,128)S(1)} fusion(s32[8,128]{1,0:T(8,128)} %param.27), kind=kOutput, calls=%fused_computation.25 | convolution fusion | flops 99328 | bytes 4352 | tf_op jit(solution)/shard_map/dot_general | solution.py:295
  3.3 0.9 %bitcast_reduce_fusion = f32[8,128]{1,0:T(8,128)S(1)} fusion(bf16[128,8,64]{0,2,1:T(8,128)(2,1)} %param.23), kind=kLoop, calls=%fused_computation.1 | loop fusion | flops 130048 | bytes 135168 | tf_op jit(solution)/shard_map/reduce_sum | solution.py:19
  4.2 0.0 copy-done.4
  4.3 0.0 copy-start.6
  4.3 0.0 copy-start.11
  4.3 0.7 %copy-done.6 = bf16[8,384]{1,0:T(8,128)(2,1)S(1)} copy-done((bf16[8,384]{1,0:T(8,128)(2,1)S(1)}, bf16[8,384]{1,0:T(8,128)(2,1)}, u32[]{:S(2)}) %copy-start.6) | copy-done | bytes 6168
  5.0 0.0 copy-done.11
  5.0 0.0 copy-start.10
  5.0 0.1 fusion.16.single_in.normed_mine
  5.1 0.6 %copy-done.10 = s32[128]{0:T(128)S(1)} copy-done((s32[128]{0:T(128)S(1)}, s32[128]{0:T(128)}, u32[]{:S(2)}) %copy-start.10) | copy-done | bytes 536
  5.7 0.0 copy-start.3
  5.7 0.0 copy-start.7
  5.7 0.1 iota_compare_fusion
  5.8 0.6 %copy-done.7 = s32[8,128]{1,0:T(8,128)S(1)} copy-done((s32[8,128]{1,0:T(8,128)S(1)}, s32[8,128]{1,0:T(8,128)}, u32[]{:S(2)}) %copy-start.7) | copy-done | bytes 4120
  6.4 0.1 fusion.21
  6.5 0.2 fusion.26
  6.7 0.0 copy-start.9
  6.7 0.8 %fusion.23.counts = f32[128,8]{1,0:T(8,128)} fusion(f32[128,8]{1,0:T(8,128)S(1)} %fusion.26, pred[128,8]{1,0:T(8,128)(4,1)S(1)} %iota_compare_fusion, s32[]{:T(128)S(6)} %select_n.3), kind=kOutput, calls=%fused_computation.30 | convolution fusion | flops 98304 | bytes 70660 | tf_op jit(solution)/shard_map/dot_general | solution.py:296
  7.5 0.0 copy-done
  7.5 0.0 copy-done.9
  7.5 0.0 copy-start.8
  7.5 0.2 fusion.8
  7.7 0.5 %copy-done.8 = bf16[64,32]{0,1:T(8,128)(2,1)S(1)} copy-done((bf16[64,32]{0,1:T(8,128)(2,1)S(1)}, bf16[64,32]{0,1:T(8,128)(2,1)}, u32[]{:S(2)}) %copy-start.8) | copy-done | bytes 4120
  8.2 0.2 fusion.10
  8.4 0.2 fusion.7
  8.6 0.0 copy-start.5
  8.6 0.9 %copy.30 = bf16[8,128,32]{2,1,0:T(8,128)(2,1)} copy(bf16[8,128,32]{1,0,2:T(8,128)(2,1)S(1)} %get-tuple-element.7) | data formatting | bytes 131072 | tf_op jit(solution)/shard_map/convert_element_type | solution.py:311
  9.5 0.1 copy-done.5
  9.6 0.1 reshape.47
  9.7 0.8 %copy.44 = bf16[32,16,256]{2,0,1:T(8,128)(2,1)} copy(bf16[32,16,256]{2,1,0:T(8,128)(2,1)S(1)} %reshape.47) | data formatting | bytes 524288 | tf_op jit(solution)/shard_map/reshape | solution.py:323
  10.4 0.0 copy-done.3
  10.4 18.5 %gather.1 = (bf16[32,16,8,128]{3,2,1,0:T(8,128)(2,1)S(1)}, bf16[16,8,384]{2,1,0:T(8,128)(2,1)S(1)}) custom-call(bf16[32,8,128]{2,1,0:T(8,128)(2,1)S(1)} %get-tuple-element.6.right_in, bf16[8,384]{1,0:T(8,128)(2,1)S(1)} %fusion.16.single_in.normed_mine), custom_call_target="tpu_custom_call" | custom-call | tf_op jit(solution)/shard_map/gather/pallas_call | solution.py:115
  28.9 0.0 copy-start.1
  28.9 1.0 %copy-done.1 = bf16[32,16,8,128]{3,2,1,0:T(8,128)(2,1)} copy-done((bf16[32,16,8,128]{3,2,1,0:T(8,128)(2,1)}, bf16[32,16,8,128]{3,2,1,0:T(8,128)(2,1)S(1)}, u32[]{:S(2)}) %copy-start.1) | copy-done | bytes 1048600
  29.9 0.0 copy-start.2
  29.9 0.6 %copy-done.2 = bf16[16,8,384]{2,1,0:T(8,128)(2,1)} copy-done((bf16[16,8,384]{2,1,0:T(8,128)(2,1)}, bf16[16,8,384]{2,1,0:T(8,128)(2,1)S(1)}, u32[]{:S(2)}) %copy-start.2) | copy-done | bytes 98328
  30.5 15.2 %finish.1 = (bf16[8,128,128]{2,1,0:T(8,128)(2,1)}, bf16[8,384]{1,0:T(8,128)(2,1)}) custom-call(bf16[1024,32]{1,0:T(8,128)(2,1)} %bitcast.38, bf16[32,128,128]{2,1,0:T(8,128)(2,1)} %bitcast.36, f32[128,8]{1,0:T(8,128)} %fusion.23.counts, bf16[8,128,128]{2,1,0:T(8,128)(2,1)} %edge.1, bf16[16,32,256]{2,1,0:T(8,128)(2,1)} %bitcast.39, f32[1,128]{1,0:T(1,128)} %bitcast.41, ...), custom_call_target="tpu_custom_call" | custom-call | tf_op jit(solution)/shard_map/finish/pallas_call | solution.py:238
  (5 shorter events, 0.1 us)
Async XLA Ops:
  0.6 6.9 %copy-start = (bf16[64,32]{0,1:T(8,128)(2,1)S(1)}, bf16[64,32]{0,1:T(8,128)(2,1)}, u32[]{:S(2)}) copy-start(bf16[64,32]{0,1:T(8,128)(2,1)} %param.30) | copy-start | bytes 12292
  0.6 3.6 %copy-start.4 = (bf16[128,8,64]{0,2,1:T(8,128)(2,1)S(1)}, bf16[128,8,64]{0,2,1:T(8,128)(2,1)}, u32[]{:S(2)}) copy-start(bf16[128,8,64]{0,2,1:T(8,128)(2,1)} %param.23) | copy-start | bytes 393220
  4.3 0.7 %copy-start.6 = (bf16[8,384]{1,0:T(8,128)(2,1)S(1)}, bf16[8,384]{1,0:T(8,128)(2,1)}, u32[]{:S(2)}) copy-start(bf16[8,384]{1,0:T(8,128)(2,1)} %residue.1) | copy-start | bytes 18436
  4.3 0.7 %copy-start.11 = (f32[384]{0:T(512)S(1)}, f32[384]{0:T(512)}, u32[]{:S(2)}) copy-start(f32[384]{0:T(512)} %param.40) | copy-start | bytes 4612
  5.0 0.7 %copy-start.10 = (s32[128]{0:T(128)S(1)}, s32[128]{0:T(128)}, u32[]{:S(2)}) copy-start(s32[128]{0:T(128)} %param.26) | copy-start | bytes 1540
  5.7 4.8 %copy-start.3 = (bf16[8,384]{1,0:T(8,128)(2,1)}, bf16[8,384]{1,0:T(8,128)(2,1)S(1)}, u32[]{:S(2)}) copy-start(bf16[8,384]{1,0:T(8,128)(2,1)S(1)} %fusion.16.single_in.normed_mine) | copy-start | bytes 18436
  5.7 0.7 %copy-start.7 = (s32[8,128]{1,0:T(8,128)S(1)}, s32[8,128]{1,0:T(8,128)}, u32[]{:S(2)}) copy-start(s32[8,128]{1,0:T(8,128)} %param.27) | copy-start | bytes 12292
  6.7 0.8 %copy-start.9 = (f32[64]{0:T(128)S(1)}, f32[64]{0:T(128)}, u32[]{:S(2)}) copy-start(f32[64]{0:T(128)} %param.29) | copy-start | bytes 772
  7.5 0.7 %copy-start.8 = (bf16[64,32]{0,1:T(8,128)(2,1)S(1)}, bf16[64,32]{0,1:T(8,128)(2,1)}, u32[]{:S(2)}) copy-start(bf16[64,32]{0,1:T(8,128)(2,1)} %param.31) | copy-start | bytes 12292
  8.6 1.0 %copy-start.5 = (bf16[1024,128]{1,0:T(8,128)(2,1)S(1)}, bf16[1024,128]{1,0:T(8,128)(2,1)}, u32[]{:S(2)}) copy-start(bf16[1024,128]{1,0:T(8,128)(2,1)} %param.32) | copy-start | bytes 786436
  28.9 1.0 %copy-start.1 = (bf16[32,16,8,128]{3,2,1,0:T(8,128)(2,1)}, bf16[32,16,8,128]{3,2,1,0:T(8,128)(2,1)S(1)}, u32[]{:S(2)}) copy-start(bf16[32,16,8,128]{3,2,1,0:T(8,128)(2,1)S(1)} %get-tuple-element.4) | copy-start | bytes 3145732
  29.9 0.6 %copy-start.2 = (bf16[16,8,384]{2,1,0:T(8,128)(2,1)}, bf16[16,8,384]{2,1,0:T(8,128)(2,1)S(1)}, u32[]{:S(2)}) copy-start(bf16[16,8,384]{2,1,0:T(8,128)(2,1)S(1)} %get-tuple-element.5) | copy-start | bytes 294916

commit v2 on v1

v2 whole, which is shorter than its diff:
```python
import functools
import math

import jax
import jax.numpy as jnp
from jax import lax
from jax.experimental import pallas as pl
from jax.experimental.pallas import tpu as pltpu
from jax.sharding import PartitionSpec as P

epsilon = 1e-05
F32 = jnp.float32
BF16 = jnp.bfloat16


def standardize_features(values, scales):
    values = values.astype(F32)
    centred = values - jnp.mean(values, axis=-1, keepdims=True)
    spread = jnp.mean(centred * centred, axis=-1, keepdims=True)
    return centred * lax.rsqrt(spread + epsilon) * scales


def digits(count):
    core = 2 if count % 2 == 0 else 1
    chips = count // core
    fast = 1
    while chips % (fast * 2) == 0 and (fast * 2) ** 2 <= chips:
        fast *= 2
    return chips // fast, fast, core


def dot(a, b):
    return jnp.dot(a, b, preferred_element_type=F32)


def dot_nt(a, b):
    return lax.dot_general(a, b, (((1,), (1,)), ((), ())), preferred_element_type=F32)


def kernel(
    count,
    alignment,
    edge,
    residue,
    labels_all,
    labels_blocks,
    membership,
    flags,
    alignment_scale,
    first,
    second,
    contraction,
    offset,
    ff_scale,
    switch,
    widening,
    narrowing,
    logit_scale,
    edge_logit,
    residue_scale,
    asking,
    lookup,
    content,
    gate_matrix,
    merge,
    pair_out,
    single_out,
    normed,
    turned,
    mine_block,
    blocks,
    mixed,
    panel,
    bias,
    divisors,
    send_sem,
    recv_sem,
):
    rows, tokens, width = edge.shape
    chains, entries = membership.shape
    factors = first.shape[1]
    heads = edge_logit.shape[0]
    single_width = residue.shape[1]
    head_size = single_width // heads
    chunks = single_width // entries

    slow, fast, core = digits(count)
    me = lax.axis_index("row")
    my_core = lax.rem(me, core)
    chip = lax.div(me, core)
    my_fast = lax.rem(chip, fast)
    my_slow = lax.div(chip, fast)

    def place(a, b, c):
        return (a * fast + b) * core + c

    slow_digits = [lax.rem(my_slow + k, slow) for k in range(slow)]
    fast_digits = [lax.rem(my_fast + k, fast) for k in range(fast)]
    other_core = lax.rem(my_core + 1, core)
    slow_peers = [place(a, my_fast, my_core) for a in slow_digits[1:]]
    fast_peers = [place(my_slow, b, my_core) for b in fast_digits[1:]]
    core_peers = [place(my_slow, my_fast, other_core)] if core == 2 else []
    peers = slow_peers + fast_peers + core_peers

    barrier = pltpu.get_barrier_semaphore()
    for peer in peers:
        pl.semaphore_signal(
            barrier, inc=1, device_id={"row": peer}, device_id_type=pl.DeviceIdType.MESH
        )

    started = []

    def block_copy(origin, peer, sent, own):
        return pltpu.make_async_remote_copy(
            src_ref=mine_block if own else blocks.at[origin],
            dst_ref=blocks.at[origin],
            send_sem=send_sem.at[sent],
            recv_sem=recv_sem.at[origin],
            device_id={"row": peer},
            device_id_type=pl.DeviceIdType.MESH,
        )

    def send(origin, targets, own=False):
        for peer in targets:
            copy = block_copy(origin, peer, len(started), own)
            copy.start()
            started.append(copy)

    def arrive(origin):
        block_copy(origin, peers[0], 0, False).wait_recv()

    normed_single = standardize_features(residue[...], residue_scale[...]).astype(BF16)
    normed[...] = standardize_features(alignment[...], alignment_scale[...])
    member = membership[...].astype(F32)
    chain_ids = lax.broadcasted_iota(jnp.int32, (chains, rows), 0)
    onehot_mine = (chain_ids == labels_blocks[pl.ds(me, 1), :]).astype(F32)
    present = jnp.concatenate(
        [
            jnp.sum(onehot_mine[:, i : i + 1] * member, axis=0, keepdims=True)
            for i in range(rows)
        ],
        axis=0,
    )
    present_columns = present.T
    lefts = []
    for i in range(rows):
        entry = normed[pl.ds(i, entries, stride=rows), :].astype(BF16)
        turned[:, i, :] = dot_nt(second[...], entry) * present[i : i + 1]
        lefts.append((dot(entry, first[...]) * present_columns[:, i : i + 1]).astype(BF16))
    mine_block[:factors] = turned[...].astype(BF16)
    for t in range(chunks):
        mine_block[factors + t] = normed_single[:, t * entries : (t + 1) * entries]

    pl.semaphore_wait(barrier, len(peers))
    send(me, peers, own=True)
    blocks[me] = mine_block[...]

    def mix(start, stop):
        for i in range(rows):
            for k in range(start, stop):
                part = dot(lefts[i], contraction[k]).astype(BF16)
                for u in range(2):
                    top = (2 * k + u) * entries
                    mixed[top : top + entries, i * width : (i + 1) * width] = part[
                        :, u * width : (u + 1) * width
                    ]

    pairs = contraction.shape[0]
    mix(0, pairs // 2)
    for a in slow_digits[1:]:
        origin = place(a, my_fast, my_core)
        arrive(origin)
        send(origin, fast_peers + core_peers)
    mix(pairs // 2, pairs)
    for b in fast_digits[1:]:
        for a in slow_digits:
            origin = place(a, b, my_core)
            arrive(origin)
            send(origin, core_peers)

    query = dot(normed_single, asking[...]).astype(BF16).astype(F32)
    gate = jax.nn.sigmoid(dot(normed_single, gate_matrix[...]))
    onehot_all = (
        lax.broadcasted_iota(jnp.int32, (chains, tokens), 0) == labels_all[...]
    ).astype(F32)
    counts = dot(dot_nt(present, member), onehot_all)
    divisors[...] = (1.0 / jnp.maximum(counts, 1.0)).T

    if core == 2:
        for b in fast_digits:
            for a in slow_digits:
                arrive(place(a, b, other_core))

    def gathered(index):
        return blocks[:, index].astype(F32).reshape(tokens, entries).astype(BF16)

    for d in range(factors):
        panel[:, d * entries : (d + 1) * entries] = gathered(d)
    normed_all = jnp.concatenate([gathered(factors + t) for t in range(chunks)], axis=1)

    step = math.gcd(tokens, 128)
    group = 2 if rows % 2 == 0 else 1
    def finish(j, carry):
        j = pl.multiple_of(j * step, step)
        for i0 in range(0, rows, group):
            update = dot(
                panel[pl.ds(j, step)], mixed[:, i0 * width : (i0 + group) * width]
            )
            for i in range(i0, i0 + group):
                part = update[:, (i - i0) * width : (i - i0 + 1) * width]
                part = part * divisors[pl.ds(j, step), i : i + 1] + offset[...]
                pair_one = (edge[i, pl.ds(j, step)].astype(F32) + part).astype(BF16)
                normed_pair = standardize_features(pair_one, ff_scale[...]).astype(BF16)
                gated = dot(normed_pair, switch[...])
                lifted = dot(normed_pair, widening[...])
                hidden = (gated / (1.0 + jnp.exp(-gated)) * lifted).astype(BF16)
                pair_two = (pair_one.astype(F32) + dot(hidden, narrowing[...])).astype(BF16)
                pair_out[i, pl.ds(j, step)] = pair_two
                bias_normed = standardize_features(pair_two, logit_scale[...]).astype(BF16)
                bias[i, :, pl.ds(j, step)] = dot_nt(edge_logit[...], bias_normed)
        return carry

    lax.fori_loop(0, tokens // step, finish, 0)

    keys = dot(normed_all, lookup[...]).astype(BF16)
    values = dot(normed_all, content[...]).astype(BF16)
    low = lax.broadcasted_iota(jnp.int32, (heads, single_width), 0) * head_size
    channel = lax.broadcasted_iota(jnp.int32, (heads, single_width), 1)
    mine = ((channel >= low) & (channel < low + head_size)).astype(F32)
    spread = jnp.concatenate([query[i : i + 1] * mine for i in range(rows)], axis=0).astype(BF16)
    scores = dot_nt(spread, keys) * (1.0 / math.sqrt(head_size)) + bias[...].reshape(
        rows * heads, tokens
    )
    live = flags[...] == 1
    scores = jnp.where(live, scores, -1e30)
    peak = jnp.max(scores, axis=-1, keepdims=True)
    expos = jnp.where(live, jnp.exp(scores - peak), 0.0)
    sums = jnp.sum(expos, axis=-1, keepdims=True)
    blended = dot(expos.astype(BF16), values) / sums
    attended = jnp.concatenate(
        [
            jnp.sum(blended[i * heads : (i + 1) * heads] * mine, axis=0, keepdims=True)
            for i in range(rows)
        ],
        axis=0,
    )
    attended = (attended * gate).astype(BF16)
    single_out[...] = (residue[...].astype(F32) + dot(attended, merge[...])).astype(BF16)
    for copy in started:
        copy.wait_send()


def local(
    sequence_features,
    edge_features,
    residue_features,
    polymer_labels,
    polymer_membership,
    present_residue_flags,
    sequence_scaling_vector,
    first_embedding_matrix,
    second_embedding_matrix,
    contraction_matrix,
    contraction_offset,
    feedforward_scaling_vector,
    feedforward_switch_matrix,
    widening_matrix,
    narrowing_matrix,
    logit_scaling_vector,
    edge_logit_matrix,
    residue_scaling_vector,
    asking_matrix,
    lookup_matrix,
    content_matrix,
    heads_sigmoid_matrix,
    heads_merge_matrix,
):
    entries, rows, depth = sequence_features.shape
    tokens, width = edge_features.shape[1:]
    factors = first_embedding_matrix.shape[1]
    heads = edge_logit_matrix.shape[1]
    count = lax.axis_size("row")
    slow, fast, core = digits(count)
    sends = (slow - 1) + slow * (fast - 1) + (slow * fast if core == 2 else 0)
    layers = factors + residue_features.shape[1] // entries
    arrays = (
        sequence_features.reshape(entries * rows, depth),
        edge_features,
        residue_features,
        polymer_labels[None],
        polymer_labels.reshape(count, rows),
        polymer_membership,
        present_residue_flags[None],
        sequence_scaling_vector[None],
        first_embedding_matrix,
        second_embedding_matrix.T,
        contraction_matrix.reshape(factors, factors // 2, 2 * width).transpose(1, 0, 2),
        contraction_offset[None],
        feedforward_scaling_vector[None],
        feedforward_switch_matrix,
        widening_matrix,
        narrowing_matrix,
        logit_scaling_vector[None],
        edge_logit_matrix.T,
        residue_scaling_vector[None],
        asking_matrix,
        lookup_matrix,
        content_matrix,
        heads_sigmoid_matrix,
        heads_merge_matrix,
    )
    return pl.pallas_call(
        functools.partial(kernel, count),
        out_shape=(
            jax.ShapeDtypeStruct(edge_features.shape, edge_features.dtype),
            jax.ShapeDtypeStruct(residue_features.shape, residue_features.dtype),
        ),
        in_specs=[pl.BlockSpec(memory_space=pltpu.VMEM)] * len(arrays),
        out_specs=(pl.BlockSpec(memory_space=pltpu.VMEM),) * 2,
        scratch_shapes=[
            pltpu.VMEM((entries * rows, depth), F32),
            pltpu.VMEM((factors, rows, entries), F32),
            pltpu.VMEM((layers, rows, entries), BF16),
            pltpu.VMEM((count, layers, rows, entries), BF16),
            pltpu.VMEM((factors * entries, rows * width), BF16),
            pltpu.VMEM((tokens, factors * entries), BF16),
            pltpu.VMEM((rows, heads, tokens), F32),
            pltpu.VMEM((tokens, rows), F32),
            pltpu.SemaphoreType.DMA((sends,)),
            pltpu.SemaphoreType.DMA((count,)),
        ],
        compiler_params=pltpu.CompilerParams(
            collective_id=0, has_side_effects=True, vmem_limit_bytes=56 * 2**20
        ),
        name="trunk",
    )(*arrays)


def solution(mesh):
    placed = (
        P("grp", "row", None),
        P(("grp", "row"), None, None),
        P(("grp", "row"), None),
        P("grp"),
        P("grp", None),
        P("grp"),
        P(),
        P(),
        P(),
        P(),
        P(),
        P(),
        P(),
        P(),
        P(),
        P(),
        P(),
        P(),
        P(),
        P(),
        P(),
        P(),
        P(),
    )
    return jax.shard_map(
        local,
        mesh=mesh,
        in_specs=placed,
        out_specs=(P(("grp", "row"), None, None), P(("grp", "row"), None)),
        check_vma=False,
    )
```

time: 46.3 us -> 38.6 us (0.83)
  Pallas kernels: 33.6 us -> 28.7 us
  local copies, waits for them, and re-layouts: 5.79 us -> 8.91 us
  other arithmetic: 3.05 us -> 0 us
  matrix products: 2.44 us -> 0 us
    pallas_call x2 -> x1, Pallas kernels: 33.6 us -> 28.7 us  [local(): pl.pallas_call(functools.partial(kernel, count), out_shape=(jax.ShapeDtyp...]
    reduce_sum x4 -> x0, other arithmetic: 2.71 us -> none  [the longest x2 1.78 us: standardize_features(): centred = values - jnp.mean(values, axis=-1, keepdims=True)]
    dot_general x6 -> x0, matrix products: 2.44 us -> none  [the longest x1 0.89 us: local(): shared = jnp.dot(membership, membership.T, precision=highest)]
    unnamed x24 -> x8, local copies, waits for them, and re-layouts: 4.05 us -> 5.43 us
    reshape x0 -> x1, local copies, waits for them, and re-layouts: none -> 1.34 us  [local(): polymer_labels.reshape(count, rows)]
    broadcast_in_dim x0 -> x1, local copies, waits for them, and re-layouts: none -> 1.29 us  [local(): residue_scaling_vector[None]]
    convert_element_type x1 -> x0, local copies, waits for them, and re-layouts: 0.86 us -> none  [local(): left = (lax.dot_general(alignment, first_embedding_matrix, (((2,), (0,)),...]
where the time goes in v2:
time: 38.6 us; the launch traced here: 38.3 us
  Pallas kernels  28.7 us (74%)
  local copies, waits for them, and re-layouts  8.91 us (23%)
  between operations  0.66 us (2%)
    pallas_call x1, Pallas kernels, local(): pl.pallas_call(functools.partial(kernel, count), out_shape=(jax.ShapeDtyp...  28.7 us
    unnamed x8, local copies, waits for them, and re-layouts  5.43 us
    reshape x1, local copies, waits for them, and re-layouts, local(): polymer_labels.reshape(count, rows)  1.34 us
    broadcast_in_dim x1, local copies, waits for them, and re-layouts, local(): residue_scaling_vector[None]  1.29 us
    reshape x2, local copies, waits for them, and re-layouts, local(): contraction_matrix.reshape(factors, factors // 2, 2 * width)  0.86 us

profile of v2, /device:TPU:1, one launch (start us, length us, event | category | flops | bytes accessed | tf_op | source)
XLA Modules:
  0.0 38.3 jit_solution(6309155110563898622)
XLA Ops:
  0.6 0.0 copy-start
  0.6 1.3 %broadcast_in_dim.27.residue_scale = f32[1,384]{1,0:T(1,128)} reshape(f32[384]{0:T(512)} %param.40) | data formatting | bytes 3072 | tf_op jit(solution)/shard_map/broadcast_in_dim | solution.py:305
  1.9 1.3 %reshape.14.labels_blocks = s32[16,8]{1,0:T(8,128)} reshape(s32[128]{0:T(128)} %param.26) | data formatting | bytes 1024 | tf_op jit(solution)/shard_map/reshape | solution.py:291
  3.3 1.4 %copy.29.first = bf16[64,32]{1,0:T(8,128)(2,1)} copy(bf16[64,32]{0,1:T(8,128)(2,1)} %param.30) | data formatting | bytes 8192 | tf_op args[7]
  4.6 1.8 %copy.27 = bf16[128,8,64]{2,1,0:T(8,128)(2,1)} copy(bf16[128,8,64]{0,2,1:T(8,128)(2,1)} %param.23) | data formatting | bytes 262144 | tf_op args[0]
  6.4 0.0 copy-done
  6.4 0.1 reshape.15
  6.5 0.8 %copy.31 = bf16[32,16,256]{2,0,1:T(8,128)(2,1)} copy(bf16[32,16,256]{2,1,0:T(8,128)(2,1)S(1)} %reshape.15) | data formatting | bytes 524288 | tf_op jit(solution)/shard_map/reshape | solution.py:297
  7.3 28.7 %trunk.1 = (bf16[8,128,128]{2,1,0:T(8,128)(2,1)}, bf16[8,384]{1,0:T(8,128)(2,1)}) custom-call(bf16[1024,64]{1,0:T(8,128)(2,1)} %bitcast.12, bf16[8,128,128]{2,1,0:T(8,128)(2,1)} %edge.1, bf16[8,384]{1,0:T(8,128)(2,1)} %residue.1, s32[1,128]{1,0:T(1,128)} %bitcast.16, s32[16,8]{1,0:T(8,128)} %reshape.14.labels_blocks, s32[8,128]{1,0:T(8,128)} %membership.1, ...), custom_call_target="tpu_custom_call" | custom-call | tf_op jit(solution)/shard_map/trunk/pallas_call | solution.py:312
  36.0 0.0 copy-start.1
  36.0 1.7 %copy.34 = bf16[8,128,128]{2,1,0:T(8,128)(2,1)} copy(bf16[8,128,128]{2,1,0:T(8,128)(2,1)} %get-tuple-element.4) | data formatting | bytes 524288
  37.7 0.0 copy-done.1
  37.7 0.6 %copy.35 = bf16[8,384]{1,0:T(8,128)(2,1)} copy(bf16[8,384]{1,0:T(8,128)(2,1)S(1)} %copy-done.1) | data formatting | bytes 12288
Async XLA Ops:
  0.6 5.8 %copy-start = (bf16[1024,128]{1,0:T(8,128)(2,1)S(1)}, bf16[1024,128]{1,0:T(8,128)(2,1)}, u32[]{:S(2)}) copy-start(bf16[1024,128]{1,0:T(8,128)(2,1)} %param.32) | copy-start | bytes 786436
  36.0 1.7 %copy-start.1 = (bf16[8,384]{1,0:T(8,128)(2,1)S(1)}, bf16[8,384]{1,0:T(8,128)(2,1)}, u32[]{:S(2)}) copy-start(bf16[8,384]{1,0:T(8,128)(2,1)} %get-tuple-element.5) | copy-start | bytes 18436

commit v3 on v2

--- a/solution.py
+++ b/solution.py
@@ -40,33 +40,43 @@
 def kernel(
     count,
     alignment,
-    edge,
+    edge_hbm,
     residue,
     labels_all,
-    labels_blocks,
     membership,
     flags,
     alignment_scale,
     first,
     second,
-    contraction,
+    contraction_hbm,
     offset,
     ff_scale,
+    switch_hbm,
+    widening_hbm,
+    narrowing_hbm,
+    logit_scale,
+    edge_logit,
+    residue_scale,
+    asking_hbm,
+    lookup_hbm,
+    content_hbm,
+    gate_matrix_hbm,
+    merge_hbm,
+    pair_out,
+    single_out,
+    turned,
+    left,
+    spread_matrix,
+    edge,
+    contraction,
     switch,
     widening,
     narrowing,
-    logit_scale,
-    edge_logit,
-    residue_scale,
     asking,
     lookup,
     content,
     gate_matrix,
     merge,
-    pair_out,
-    single_out,
-    normed,
-    turned,
     mine_block,
     blocks,
     mixed,
@@ -75,14 +85,35 @@
     divisors,
     send_sem,
     recv_sem,
+    load_sem,
 ):
-    rows, tokens, width = edge.shape
+    rows, tokens, width = edge_hbm.shape
     chains, entries = membership.shape
-    factors = first.shape[1]
+    factors = first.shape[0]
     heads = edge_logit.shape[0]
     single_width = residue.shape[1]
     head_size = single_width // heads
     chunks = single_width // entries
+
+    loads = [
+        pltpu.make_async_copy(source, target, load_sem.at[index])
+        for index, (source, target) in enumerate(
+            (
+                (contraction_hbm, contraction),
+                (asking_hbm, asking),
+                (gate_matrix_hbm, gate_matrix),
+                (edge_hbm, edge),
+                (switch_hbm, switch),
+                (widening_hbm, widening),
+                (narrowing_hbm, narrowing),
+                (lookup_hbm, lookup),
+                (content_hbm, content),
+                (merge_hbm, merge),
+            )
+        )
+    ]
+    for load in loads:
+        load.start()
 
     slow, fast, core = digits(count)
     me = lax.axis_index("row")
@@ -130,10 +161,13 @@
         block_copy(origin, peers[0], 0, False).wait_recv()
 
     normed_single = standardize_features(residue[...], residue_scale[...]).astype(BF16)
-    normed[...] = standardize_features(alignment[...], alignment_scale[...])
     member = membership[...].astype(F32)
-    chain_ids = lax.broadcasted_iota(jnp.int32, (chains, rows), 0)
-    onehot_mine = (chain_ids == labels_blocks[pl.ds(me, 1), :]).astype(F32)
+    onehot_all = (
+        lax.broadcasted_iota(jnp.int32, (chains, tokens), 0) == labels_all[...]
+    ).astype(F32)
+    here = lax.broadcasted_iota(jnp.int32, (tokens, rows), 1) + me * rows
+    chosen = (lax.broadcasted_iota(jnp.int32, (tokens, rows), 0) == here).astype(F32)
+    onehot_mine = dot(onehot_all, chosen)
     present = jnp.concatenate(
         [
             jnp.sum(onehot_mine[:, i : i + 1] * member, axis=0, keepdims=True)
@@ -141,12 +175,20 @@
         ],
         axis=0,
     )
-    present_columns = present.T
-    lefts = []
+    depth = first.shape[1]
+    diagonal = lax.broadcasted_iota(jnp.int32, (depth, depth), 0) == lax.broadcasted_iota(
+        jnp.int32, (depth, depth), 1
+    )
+    gains = jnp.sum(jnp.where(diagonal, alignment_scale[...], 0.0), axis=1, keepdims=True)
+    both = jnp.concatenate([first[...], second[...]], axis=0)
     for i in range(rows):
-        entry = normed[pl.ds(i, entries, stride=rows), :].astype(BF16)
-        turned[:, i, :] = dot_nt(second[...], entry) * present[i : i + 1]
-        lefts.append((dot(entry, first[...]) * present_columns[:, i : i + 1]).astype(BF16))
+        entry = alignment[i].astype(F32)
+        entry = entry - jnp.mean(entry, axis=0, keepdims=True)
+        variance = jnp.mean(entry * entry, axis=0, keepdims=True)
+        entry = (entry * lax.rsqrt(variance + epsilon) * gains).astype(BF16)
+        embedded = dot(both, entry) * present[i : i + 1]
+        turned[:, i, :] = embedded[factors:]
+        left[i] = embedded[:factors].T.astype(BF16)
     mine_block[:factors] = turned[...].astype(BF16)
     for t in range(chunks):
         mine_block[factors + t] = normed_single[:, t * entries : (t + 1) * entries]
@@ -155,17 +197,27 @@
     send(me, peers, own=True)
     blocks[me] = mine_block[...]
 
+    loads[0].wait()
+    spread_matrix[...] = contraction[...].astype(F32)
+
     def mix(start, stop):
-        for i in range(rows):
-            for k in range(start, stop):
-                part = dot(lefts[i], contraction[k]).astype(BF16)
+        for k in range(start, stop):
+            panels = jnp.concatenate(
+                [
+                    spread_matrix[pl.ds(2 * k + u, factors, stride=factors), :]
+                    for u in range(2)
+                ],
+                axis=1,
+            ).astype(BF16)
+            for i in range(rows):
+                part = dot(left[i], panels).astype(BF16)
                 for u in range(2):
                     top = (2 * k + u) * entries
                     mixed[top : top + entries, i * width : (i + 1) * width] = part[
                         :, u * width : (u + 1) * width
                     ]
 
-    pairs = contraction.shape[0]
+    pairs = factors // 2
     mix(0, pairs // 2)
     for a in slow_digits[1:]:
         origin = place(a, my_fast, my_core)
@@ -178,11 +230,10 @@
             arrive(origin)
             send(origin, core_peers)
 
+    loads[1].wait()
+    loads[2].wait()
     query = dot(normed_single, asking[...]).astype(BF16).astype(F32)
     gate = jax.nn.sigmoid(dot(normed_single, gate_matrix[...]))
-    onehot_all = (
-        lax.broadcasted_iota(jnp.int32, (chains, tokens), 0) == labels_all[...]
-    ).astype(F32)
     counts = dot(dot_nt(present, member), onehot_all)
     divisors[...] = (1.0 / jnp.maximum(counts, 1.0)).T
 
@@ -198,6 +249,8 @@
         panel[:, d * entries : (d + 1) * entries] = gathered(d)
     normed_all = jnp.concatenate([gathered(factors + t) for t in range(chunks)], axis=1)
 
+    for load in loads[3:]:
+        load.wait()
     step = math.gcd(tokens, 128)
     group = 2 if rows % 2 == 0 else 1
     def finish(j, carry):
@@ -275,7 +328,7 @@
     heads_sigmoid_matrix,
     heads_merge_matrix,
 ):
-    entries, rows, depth = sequence_features.shape
+    entries, rows, _ = sequence_features.shape
     tokens, width = edge_features.shape[1:]
     factors = first_embedding_matrix.shape[1]
     heads = edge_logit_matrix.shape[1]
@@ -284,17 +337,16 @@
     sends = (slow - 1) + slow * (fast - 1) + (slow * fast if core == 2 else 0)
     layers = factors + residue_features.shape[1] // entries
     arrays = (
-        sequence_features.reshape(entries * rows, depth),
+        sequence_features.transpose(1, 2, 0),
         edge_features,
         residue_features,
         polymer_labels[None],
-        polymer_labels.reshape(count, rows),
         polymer_membership,
         present_residue_flags[None],
         sequence_scaling_vector[None],
-        first_embedding_matrix,
+        first_embedding_matrix.T,
         second_embedding_matrix.T,
-        contraction_matrix.reshape(factors, factors // 2, 2 * width).transpose(1, 0, 2),
+        contraction_matrix,
         contraction_offset[None],
         feedforward_scaling_vector[None],
         feedforward_switch_matrix,
@@ -302,24 +354,39 @@
         narrowing_matrix,
         logit_scaling_vector[None],
         edge_logit_matrix.T,
-        residue_scaling_vector[None],
+        residue_scaling_vector,
         asking_matrix,
         lookup_matrix,
         content_matrix,
         heads_sigmoid_matrix,
         heads_merge_matrix,
     )
+    large = (1, 9, 12, 13, 14, 18, 19, 20, 21, 22)
     return pl.pallas_call(
         functools.partial(kernel, count),
         out_shape=(
             jax.ShapeDtypeStruct(edge_features.shape, edge_features.dtype),
             jax.ShapeDtypeStruct(residue_features.shape, residue_features.dtype),
         ),
-        in_specs=[pl.BlockSpec(memory_space=pltpu.VMEM)] * len(arrays),
+        in_specs=[
+            pl.BlockSpec(memory_space=pl.ANY if index in large else pltpu.VMEM)
+            for index in range(len(arrays))
+        ],
         out_specs=(pl.BlockSpec(memory_space=pltpu.VMEM),) * 2,
         scratch_shapes=[
-            pltpu.VMEM((entries * rows, depth), F32),
             pltpu.VMEM((factors, rows, entries), F32),
+            pltpu.VMEM((rows, entries, factors), BF16),
+            pltpu.VMEM(contraction_matrix.shape, F32),
+            pltpu.VMEM(arrays[1].shape, BF16),
+            pltpu.VMEM(arrays[9].shape, BF16),
+            pltpu.VMEM(arrays[12].shape, BF16),
+            pltpu.VMEM(arrays[13].shape, BF16),
+            pltpu.VMEM(arrays[14].shape, BF16),
+            pltpu.VMEM(arrays[18].shape, BF16),
+            pltpu.VMEM(arrays[19].shape, BF16),
+            pltpu.VMEM(arrays[20].shape, BF16),
+            pltpu.VMEM(arrays[21].shape, BF16),
+            pltpu.VMEM(arrays[22].shape, BF16),
             pltpu.VMEM((layers, rows, entries), BF16),
             pltpu.VMEM((count, layers, rows, entries), BF16),
             pltpu.VMEM((factors * entries, rows * width), BF16),
@@ -328,9 +395,10 @@
             pltpu.VMEM((tokens, rows), F32),
             pltpu.SemaphoreType.DMA((sends,)),
             pltpu.SemaphoreType.DMA((count,)),
+            pltpu.SemaphoreType.DMA((len(large),)),
         ],
         compiler_params=pltpu.CompilerParams(
-            collective_id=0, has_side_effects=True, vmem_limit_bytes=56 * 2**20
+            collective_id=0, has_side_effects=True, vmem_limit_bytes=44 * 2**20
         ),
         name="trunk",
     )(*arrays)

time: 38.6 us -> 46.3 us (1.20)
  local copies, waits for them, and re-layouts: 8.91 us -> 17.7 us
  Pallas kernels: 28.7 us -> 27.3 us
    unnamed x8 -> x48, local copies, waits for them, and re-layouts: 5.43 us -> 17.7 us
    reshape x3 -> x0, local copies, waits for them, and re-layouts: 2.19 us -> none  [the longest x1 1.34 us: local(): polymer_labels.reshape(count, rows)]
    pallas_call x1, Pallas kernels: 28.7 us -> 27.3 us  [local(): pl.pallas_call(functools.partial(kernel, count), out_shape=(jax.ShapeDtyp...]
    broadcast_in_dim x1 -> x0, local copies, waits for them, and re-layouts: 1.29 us -> none  [local(): residue_scaling_vector[None]]
where the time goes in v3:
time: 46.3 us; the launch traced here: 45.7 us
  Pallas kernels  27.3 us (59%)
  local copies, waits for them, and re-layouts  17.7 us (38%)
  between operations  0.7 us (2%)
    pallas_call x1, Pallas kernels, local(): pl.pallas_call(functools.partial(kernel, count), out_shape=(jax.ShapeDtyp...  27.3 us
    unnamed x48, local copies, waits for them, and re-layouts  17.7 us

profile of v3, /device:TPU:1, one launch (start us, length us, event | category | flops | bytes accessed | tf_op | source)
XLA Modules:
  0.0 45.7 jit_solution(6952680989210718496)
XLA Ops:
  0.6 0.0 copy-start.16
  0.6 0.0 copy-start.12
  0.7 0.0 copy-start.11
  0.7 0.0 copy-start.17
  0.7 0.6 %copy-done.16 = f32[384]{0:T(512)S(1)} copy-done((f32[384]{0:T(512)S(1)}, f32[384]{0:T(512)}, u32[]{:S(2)}) %copy-start.16) | copy-done | bytes 1560
  1.3 0.0 copy-done.12
  1.4 0.0 copy-done.11
  1.4 0.0 copy-done.17
  1.4 1.0 %copy-done = bf16[384,384]{1,0:T(8,128)(2,1)S(1)} copy-done((bf16[384,384]{1,0:T(8,128)(2,1)S(1)}, bf16[384,384]{1,0:T(8,128)(2,1)}, u32[]{:S(2)}) %copy-start) | copy-done | bytes 294936
  2.3 0.0 copy-start.1
  2.3 1.0 %copy-done.1 = bf16[384,384]{1,0:T(8,128)(2,1)S(1)} copy-done((bf16[384,384]{1,0:T(8,128)(2,1)S(1)}, bf16[384,384]{1,0:T(8,128)(2,1)}, u32[]{:S(2)}) %copy-start.1) | copy-done | bytes 294936
  3.3 0.0 copy-start.2
  3.3 1.0 %copy-done.2 = bf16[384,384]{1,0:T(8,128)(2,1)S(1)} copy-done((bf16[384,384]{1,0:T(8,128)(2,1)S(1)}, bf16[384,384]{1,0:T(8,128)(2,1)}, u32[]{:S(2)}) %copy-start.2) | copy-done | bytes 294936
  4.3 0.0 copy-start.3
  4.3 1.0 %copy-done.3 = bf16[384,384]{1,0:T(8,128)(2,1)S(1)} copy-done((bf16[384,384]{1,0:T(8,128)(2,1)S(1)}, bf16[384,384]{1,0:T(8,128)(2,1)}, u32[]{:S(2)}) %copy-start.3) | copy-done | bytes 294936
  5.2 0.0 copy-start.4
  5.2 1.0 %copy-done.4 = bf16[384,384]{1,0:T(8,128)(2,1)S(1)} copy-done((bf16[384,384]{1,0:T(8,128)(2,1)S(1)}, bf16[384,384]{1,0:T(8,128)(2,1)}, u32[]{:S(2)}) %copy-start.4) | copy-done | bytes 294936
  6.2 0.0 copy-start.5
  6.2 0.9 %copy-done.5 = bf16[8,128,128]{2,1,0:T(8,128)(2,1)S(1)} copy-done((bf16[8,128,128]{2,1,0:T(8,128)(2,1)S(1)}, bf16[8,128,128]{2,1,0:T(8,128)(2,1)}, u32[]{:S(2)}) %copy-start.5) | copy-done | bytes 262168
  7.1 0.0 copy-start.6
  7.1 0.9 %copy-done.6 = bf16[1024,128]{1,0:T(8,128)(2,1)S(1)} copy-done((bf16[1024,128]{1,0:T(8,128)(2,1)S(1)}, bf16[1024,128]{1,0:T(8,128)(2,1)}, u32[]{:S(2)}) %copy-start.6) | copy-done | bytes 262168
  8.1 0.0 copy-start.7
  8.1 0.9 %copy-done.7 = bf16[128,8,64]{0,2,1:T(8,128)(2,1)S(1)} copy-done((bf16[128,8,64]{0,2,1:T(8,128)(2,1)S(1)}, bf16[128,8,64]{0,2,1:T(8,128)(2,1)}, u32[]{:S(2)}) %copy-start.7) | copy-done | bytes 131096
  9.0 0.0 copy-start.8
  9.0 0.9 %copy-done.8 = bf16[128,512]{1,0:T(8,128)(2,1)S(1)} copy-done((bf16[128,512]{1,0:T(8,128)(2,1)S(1)}, bf16[128,512]{1,0:T(8,128)(2,1)}, u32[]{:S(2)}) %copy-start.8) | copy-done | bytes 131096
  9.9 0.0 copy-start.9
  9.9 0.9 %copy-done.9 = bf16[128,512]{1,0:T(8,128)(2,1)S(1)} copy-done((bf16[128,512]{1,0:T(8,128)(2,1)S(1)}, bf16[128,512]{1,0:T(8,128)(2,1)}, u32[]{:S(2)}) %copy-start.9) | copy-done | bytes 131096
  10.8 0.0 copy-start.10
  10.8 0.9 %copy-done.10 = bf16[512,128]{1,0:T(8,128)(2,1)S(1)} copy-done((bf16[512,128]{1,0:T(8,128)(2,1)S(1)}, bf16[512,128]{1,0:T(8,128)(2,1)}, u32[]{:S(2)}) %copy-start.10) | copy-done | bytes 131096
  11.7 0.0 copy-start.13
  11.7 0.7 %copy-done.13 = bf16[8,384]{1,0:T(8,128)(2,1)S(1)} copy-done((bf16[8,384]{1,0:T(8,128)(2,1)S(1)}, bf16[8,384]{1,0:T(8,128)(2,1)}, u32[]{:S(2)}) %copy-start.13) | copy-done | bytes 6168
  12.4 0.0 copy-start.14
  12.4 0.7 %copy-done.14 = s32[8,128]{1,0:T(8,128)S(1)} copy-done((s32[8,128]{1,0:T(8,128)S(1)}, s32[8,128]{1,0:T(8,128)}, u32[]{:S(2)}) %copy-start.14) | copy-done | bytes 4120
  13.1 0.0 copy-start.15
  13.1 0.7 %copy-done.15 = bf16[128,16]{0,1:T(8,128)(2,1)S(1)} copy-done((bf16[128,16]{0,1:T(8,128)(2,1)S(1)}, bf16[128,16]{0,1:T(8,128)(2,1)}, u32[]{:S(2)}) %copy-start.15) | copy-done | bytes 4120
  13.8 0.0 copy-start.18
  13.8 0.7 %copy-done.18 = s32[128]{0:T(128)S(1)} copy-done((s32[128]{0:T(128)S(1)}, s32[128]{0:T(128)}, u32[]{:S(2)}) %copy-start.18) | copy-done | bytes 536
  14.4 0.0 copy-start.19
  14.4 0.7 %copy-done.19 = f32[64]{0:T(128)S(1)} copy-done((f32[64]{0:T(128)S(1)}, f32[64]{0:T(128)}, u32[]{:S(2)}) %copy-start.19) | copy-done | bytes 280
  15.1 0.0 copy-start.20
  15.1 0.7 %copy-done.20 = f32[128]{0:T(128)S(1)} copy-done((f32[128]{0:T(128)S(1)}, f32[128]{0:T(128)}, u32[]{:S(2)}) %copy-start.20) | copy-done | bytes 536
  15.7 0.0 copy-start.21
  15.7 0.7 %copy-done.21 = f32[128]{0:T(128)S(1)} copy-done((f32[128]{0:T(128)S(1)}, f32[128]{0:T(128)}, u32[]{:S(2)}) %copy-start.21) | copy-done | bytes 536
  16.4 0.0 copy-start.22
  16.4 0.7 %copy-done.22 = f32[128]{0:T(128)S(1)} copy-done((f32[128]{0:T(128)S(1)}, f32[128]{0:T(128)}, u32[]{:S(2)}) %copy-start.22) | copy-done | bytes 536
  17.0 27.3 %trunk.1 = (bf16[8,128,128]{2,1,0:T(8,128)(2,1)S(1)}, bf16[8,384]{1,0:T(8,128)(2,1)S(1)}) custom-call(bf16[8,64,128]{2,1,0:T(8,128)(2,1)S(1)} %bitcast.10, bf16[8,128,128]{2,1,0:T(8,128)(2,1)S(1)} %copy-done.5, bf16[8,384]{1,0:T(8,128)(2,1)S(1)} %copy-done.13, s32[1,128]{1,0:T(1,128)S(1)} %bitcast.14, s32[8,128]{1,0:T(8,128)S(1)} %copy-done.14, ...), custom_call_target="tpu_custom_call" | custom-call | tf_op jit(solution)/shard_map/trunk/pallas_call | solution.py:365
  44.4 0.7 %copy.27 = bf16[8,128,128]{2,1,0:T(8,128)(2,1)} copy(bf16[8,128,128]{2,1,0:T(8,128)(2,1)S(1)} %get-tuple-element.4) | data formatting | bytes 524288
  45.1 0.6 %copy.28 = bf16[8,384]{1,0:T(8,128)(2,1)} copy(bf16[8,384]{1,0:T(8,128)(2,1)S(1)} %get-tuple-element.5) | data formatting | bytes 12288
  (1 shorter events, 0.0 us)
Async XLA Ops:
  0.6 0.7 %copy-start.16 = (f32[384]{0:T(512)S(1)}, f32[384]{0:T(512)}, u32[]{:S(2)}) copy-start(f32[384]{0:T(512)} %residue_scale.1) | copy-start | bytes 4612
  0.6 0.7 %copy-start.12 = (bf16[64,32]{0,1:T(8,128)(2,1)S(1)}, bf16[64,32]{0,1:T(8,128)(2,1)}, u32[]{:S(2)}) copy-start(bf16[64,32]{0,1:T(8,128)(2,1)} %param.31) | copy-start | bytes 12292
  0.7 0.7 %copy-start.11 = (bf16[64,32]{0,1:T(8,128)(2,1)S(1)}, bf16[64,32]{0,1:T(8,128)(2,1)}, u32[]{:S(2)}) copy-start(bf16[64,32]{0,1:T(8,128)(2,1)} %param.30) | copy-start | bytes 12292
  0.7 0.7 %copy-start.17 = (s32[128]{0:T(128)S(1)}, s32[128]{0:T(128)}, u32[]{:S(2)}) copy-start(s32[128]{0:T(128)} %param.26) | copy-start | bytes 1540
  1.4 1.0 %copy-start = (bf16[384,384]{1,0:T(8,128)(2,1)S(1)}, bf16[384,384]{1,0:T(8,128)(2,1)}, u32[]{:S(2)}) copy-start(bf16[384,384]{1,0:T(8,128)(2,1)} %asking_hbm.1) | copy-start | bytes 884740
  2.3 1.0 %copy-start.1 = (bf16[384,384]{1,0:T(8,128)(2,1)S(1)}, bf16[384,384]{1,0:T(8,128)(2,1)}, u32[]{:S(2)}) copy-start(bf16[384,384]{1,0:T(8,128)(2,1)} %lookup_hbm.1) | copy-start | bytes 884740
  3.3 1.0 %copy-start.2 = (bf16[384,384]{1,0:T(8,128)(2,1)S(1)}, bf16[384,384]{1,0:T(8,128)(2,1)}, u32[]{:S(2)}) copy-start(bf16[384,384]{1,0:T(8,128)(2,1)} %content_hbm.1) | copy-start | bytes 884740
  4.3 1.0 %copy-start.3 = (bf16[384,384]{1,0:T(8,128)(2,1)S(1)}, bf16[384,384]{1,0:T(8,128)(2,1)}, u32[]{:S(2)}) copy-start(bf16[384,384]{1,0:T(8,128)(2,1)} %gate_matrix_hbm.1) | copy-start | bytes 884740
  5.2 1.0 %copy-start.4 = (bf16[384,384]{1,0:T(8,128)(2,1)S(1)}, bf16[384,384]{1,0:T(8,128)(2,1)}, u32[]{:S(2)}) copy-start(bf16[384,384]{1,0:T(8,128)(2,1)} %merge_hbm.1) | copy-start | bytes 884740
  6.2 0.9 %copy-start.5 = (bf16[8,128,128]{2,1,0:T(8,128)(2,1)S(1)}, bf16[8,128,128]{2,1,0:T(8,128)(2,1)}, u32[]{:S(2)}) copy-start(bf16[8,128,128]{2,1,0:T(8,128)(2,1)} %edge_hbm.1) | copy-start | bytes 786436
  7.1 0.9 %copy-start.6 = (bf16[1024,128]{1,0:T(8,128)(2,1)S(1)}, bf16[1024,128]{1,0:T(8,128)(2,1)}, u32[]{:S(2)}) copy-start(bf16[1024,128]{1,0:T(8,128)(2,1)} %contraction_hbm.1) | copy-start | bytes 786436
  8.1 0.9 %copy-start.7 = (bf16[128,8,64]{0,2,1:T(8,128)(2,1)S(1)}, bf16[128,8,64]{0,2,1:T(8,128)(2,1)}, u32[]{:S(2)}) copy-start(bf16[128,8,64]{0,2,1:T(8,128)(2,1)} %param.23) | copy-start | bytes 393220
  9.0 0.9 %copy-start.8 = (bf16[128,512]{1,0:T(8,128)(2,1)S(1)}, bf16[128,512]{1,0:T(8,128)(2,1)}, u32[]{:S(2)}) copy-start(bf16[128,512]{1,0:T(8,128)(2,1)} %switch_hbm.1) | copy-start | bytes 393220
  9.9 0.9 %copy-start.9 = (bf16[128,512]{1,0:T(8,128)(2,1)S(1)}, bf16[128,512]{1,0:T(8,128)(2,1)}, u32[]{:S(2)}) copy-start(bf16[128,512]{1,0:T(8,128)(2,1)} %widening_hbm.1) | copy-start | bytes 393220
  10.8 0.9 %copy-start.10 = (bf16[512,128]{1,0:T(8,128)(2,1)S(1)}, bf16[512,128]{1,0:T(8,128)(2,1)}, u32[]{:S(2)}) copy-start(bf16[512,128]{1,0:T(8,128)(2,1)} %narrowing_hbm.1) | copy-start | bytes 393220
  11.7 0.7 %copy-start.13 = (bf16[8,384]{1,0:T(8,128)(2,1)S(1)}, bf16[8,384]{1,0:T(8,128)(2,1)}, u32[]{:S(2)}) copy-start(bf16[8,384]{1,0:T(8,128)(2,1)} %residue.1) | copy-start | bytes 18436
  12.4 0.7 %copy-start.14 = (s32[8,128]{1,0:T(8,128)S(1)}, s32[8,128]{1,0:T(8,128)}, u32[]{:S(2)}) copy-start(s32[8,128]{1,0:T(8,128)} %membership.1) | copy-start | bytes 12292
  13.1 0.7 %copy-start.15 = (bf16[128,16]{0,1:T(8,128)(2,1)S(1)}, bf16[128,16]{0,1:T(8,128)(2,1)}, u32[]{:S(2)}) copy-start(bf16[128,16]{0,1:T(8,128)(2,1)} %param.39) | copy-start | bytes 12292
  13.8 0.7 %copy-start.18 = (s32[128]{0:T(128)S(1)}, s32[128]{0:T(128)}, u32[]{:S(2)}) copy-start(s32[128]{0:T(128)} %param.28) | copy-start | bytes 1540
  14.4 0.7 %copy-start.19 = (f32[64]{0:T(128)S(1)}, f32[64]{0:T(128)}, u32[]{:S(2)}) copy-start(f32[64]{0:T(128)} %param.29) | copy-start | bytes 772
  15.1 0.7 %copy-start.20 = (f32[128]{0:T(128)S(1)}, f32[128]{0:T(128)}, u32[]{:S(2)}) copy-start(f32[128]{0:T(128)} %param.33) | copy-start | bytes 1540
  15.7 0.7 %copy-start.21 = (f32[128]{0:T(128)S(1)}, f32[128]{0:T(128)}, u32[]{:S(2)}) copy-start(f32[128]{0:T(128)} %param.34) | copy-start | bytes 1540
  16.4 0.7 %copy-start.22 = (f32[128]{0:T(128)S(1)}, f32[128]{0:T(128)}, u32[]{:S(2)}) copy-start(f32[128]{0:T(128)} %param.38) | copy-start | bytes 1540

commit v4 on v3

--- a/solution.py
+++ b/solution.py
@@ -398,7 +398,7 @@
             pltpu.SemaphoreType.DMA((len(large),)),
         ],
         compiler_params=pltpu.CompilerParams(
-            collective_id=0, has_side_effects=True, vmem_limit_bytes=44 * 2**20
+            collective_id=0, has_side_effects=True, vmem_limit_bytes=56 * 2**20
         ),
         name="trunk",
     )(*arrays)

time: 46.3 us -> 31.3 us (0.68)
  local copies, waits for them, and re-layouts: 17.7 us -> 2.27 us
  Pallas kernels: 27.3 us -> 28.2 us
    unnamed x48 -> x4, local copies, waits for them, and re-layouts: 17.7 us -> 2.27 us
    pallas_call x1, Pallas kernels: 27.3 us -> 28.2 us  [local(): pl.pallas_call(functools.partial(kernel, count), out_shape=(jax.ShapeDtyp...]
where the time goes in v4:
time: 31.3 us; the launch traced here: 31.1 us
  Pallas kernels  28.2 us (90%)
  local copies, waits for them, and re-layouts  2.27 us (7%)
  between operations  0.66 us (2%)
    pallas_call x1, Pallas kernels, local(): pl.pallas_call(functools.partial(kernel, count), out_shape=(jax.ShapeDtyp...  28.2 us
    unnamed x4, local copies, waits for them, and re-layouts  2.27 us

profile of v4, /device:TPU:1, one launch (start us, length us, event | category | flops | bytes accessed | tf_op | source)
XLA Modules:
  0.0 31.1 jit_solution(10565019600838878636)
XLA Ops:
  0.6 28.2 %trunk.1 = (bf16[8,128,128]{2,1,0:T(8,128)(2,1)}, bf16[8,384]{1,0:T(8,128)(2,1)}) custom-call(bf16[8,64,128]{2,1,0:T(8,128)(2,1)} %bitcast.10, bf16[8,128,128]{2,1,0:T(8,128)(2,1)} %edge_hbm.1, bf16[8,384]{1,0:T(8,128)(2,1)} %residue.1, s32[1,128]{1,0:T(1,128)} %bitcast.14, s32[8,128]{1,0:T(8,128)} %membership.1, s32[1,128]{1,0:T(1,128)} %bitcast.15, ...), custom_call_target="tpu_custom_call" | custom-call | tf_op jit(solution)/shard_map/trunk/pallas_call | solution.py:365
  28.8 0.0 copy-start
  28.8 1.7 %copy.27 = bf16[8,128,128]{2,1,0:T(8,128)(2,1)} copy(bf16[8,128,128]{2,1,0:T(8,128)(2,1)} %get-tuple-element.4) | data formatting | bytes 524288
  30.5 0.0 copy-done
  30.5 0.6 %copy.28 = bf16[8,384]{1,0:T(8,128)(2,1)} copy(bf16[8,384]{1,0:T(8,128)(2,1)S(1)} %copy-done) | data formatting | bytes 12288
Async XLA Ops:
  28.8 1.7 %copy-start = (bf16[8,384]{1,0:T(8,128)(2,1)S(1)}, bf16[8,384]{1,0:T(8,128)(2,1)}, u32[]{:S(2)}) copy-start(bf16[8,384]{1,0:T(8,128)(2,1)} %get-tuple-element.5) | copy-start | bytes 18436

commit v5 on v4

--- a/solution.py
+++ b/solution.py
@@ -94,6 +94,7 @@
     single_width = residue.shape[1]
     head_size = single_width // heads
     chunks = single_width // entries
+    layers = factors + chunks
 
     loads = [
         pltpu.make_async_copy(source, target, load_sem.at[index])
@@ -218,17 +219,28 @@
                     ]
 
     pairs = factors // 2
-    mix(0, pairs // 2)
-    for a in slow_digits[1:]:
+    def settle(a, b):
+        base = (a * fast + b) * core
+        place_rows = pl.ds(pl.multiple_of(base * rows, core * rows), core * rows)
+        for d in range(layers):
+            layer = blocks[pl.ds(base, core), d].astype(F32)
+            panel[place_rows, d * entries : (d + 1) * entries] = layer.reshape(
+                core * rows, entries
+            ).astype(BF16)
+
+    parts = slow + 1
+    bounds = [pairs * k // parts for k in range(parts + 1)]
+    mix(bounds[0], bounds[1])
+    for k, a in enumerate(slow_digits[1:]):
         origin = place(a, my_fast, my_core)
         arrive(origin)
         send(origin, fast_peers + core_peers)
-    mix(pairs // 2, pairs)
-    for b in fast_digits[1:]:
-        for a in slow_digits:
-            origin = place(a, b, my_core)
-            arrive(origin)
-            send(origin, core_peers)
+        mix(bounds[k + 1], bounds[k + 2])
+    mix(bounds[slow], bounds[parts])
+    for a in slow_digits:
+        if core == 2:
+            arrive(place(a, my_fast, other_core))
+        settle(a, my_fast)
 
     loads[1].wait()
     loads[2].wait()
@@ -237,17 +249,17 @@
     counts = dot(dot_nt(present, member), onehot_all)
     divisors[...] = (1.0 / jnp.maximum(counts, 1.0)).T
 
-    if core == 2:
-        for b in fast_digits:
-            for a in slow_digits:
+    for b in fast_digits[1:]:
+        for a in slow_digits:
+            origin = place(a, b, my_core)
+            arrive(origin)
+            send(origin, core_peers)
+    for b in fast_digits[1:]:
+        for a in slow_digits:
+            if core == 2:
                 arrive(place(a, b, other_core))
-
-    def gathered(index):
-        return blocks[:, index].astype(F32).reshape(tokens, entries).astype(BF16)
-
-    for d in range(factors):
-        panel[:, d * entries : (d + 1) * entries] = gathered(d)
-    normed_all = jnp.concatenate([gathered(factors + t) for t in range(chunks)], axis=1)
+            settle(a, b)
+    normed_all = panel[:, factors * entries :]
 
     for load in loads[3:]:
         load.wait()
@@ -257,7 +269,7 @@
         j = pl.multiple_of(j * step, step)
         for i0 in range(0, rows, group):
             update = dot(
-                panel[pl.ds(j, step)], mixed[:, i0 * width : (i0 + group) * width]
+                panel[pl.ds(j, step), : factors * entries], mixed[:, i0 * width : (i0 + group) * width]
             )
             for i in range(i0, i0 + group):
                 part = update[:, (i - i0) * width : (i - i0 + 1) * width]
@@ -390,7 +402,7 @@
             pltpu.VMEM((layers, rows, entries), BF16),
             pltpu.VMEM((count, layers, rows, entries), BF16),
             pltpu.VMEM((factors * entries, rows * width), BF16),
-            pltpu.VMEM((tokens, factors * entries), BF16),
+            pltpu.VMEM((tokens, layers * entries), BF16),
             pltpu.VMEM((rows, heads, tokens), F32),
             pltpu.VMEM((tokens, rows), F32),
             pltpu.SemaphoreType.DMA((sends,)),

time: 31.3 us -> 31 us (level)
  no operation moved by 1% of the time
where the time goes in v5:
time: 31 us; the launch traced here: 30.9 us
  Pallas kernels  27.9 us (90%)
  local copies, waits for them, and re-layouts  2.27 us (7%)
  between operations  0.66 us (2%)
    pallas_call x1, Pallas kernels, local(): pl.pallas_call(functools.partial(kernel, count), out_shape=(jax.ShapeDtyp...  27.9 us
    unnamed x4, local copies, waits for them, and re-layouts  2.27 us

profile of v5, /device:TPU:1, one launch (start us, length us, event | category | flops | bytes accessed | tf_op | source)
XLA Modules:
  0.0 30.9 jit_solution(8136258977063639719)
XLA Ops:
  0.6 27.9 %trunk.1 = (bf16[8,128,128]{2,1,0:T(8,128)(2,1)}, bf16[8,384]{1,0:T(8,128)(2,1)}) custom-call(bf16[8,64,128]{2,1,0:T(8,128)(2,1)} %bitcast.10, bf16[8,128,128]{2,1,0:T(8,128)(2,1)} %edge_hbm.1, bf16[8,384]{1,0:T(8,128)(2,1)} %residue.1, s32[1,128]{1,0:T(1,128)} %bitcast.14, s32[8,128]{1,0:T(8,128)} %membership.1, s32[1,128]{1,0:T(1,128)} %bitcast.15, ...), custom_call_target="tpu_custom_call" | custom-call | tf_op jit(solution)/shard_map/trunk/pallas_call | solution.py:377
  28.6 0.0 copy-start
  28.6 1.7 %copy.27 = bf16[8,128,128]{2,1,0:T(8,128)(2,1)} copy(bf16[8,128,128]{2,1,0:T(8,128)(2,1)} %get-tuple-element.4) | data formatting | bytes 524288
  30.3 0.0 copy-done
  30.3 0.6 %copy.28 = bf16[8,384]{1,0:T(8,128)(2,1)} copy(bf16[8,384]{1,0:T(8,128)(2,1)S(1)} %copy-done) | data formatting | bytes 12288
Async XLA Ops:
  28.6 1.7 %copy-start = (bf16[8,384]{1,0:T(8,128)(2,1)S(1)}, bf16[8,384]{1,0:T(8,128)(2,1)}, u32[]{:S(2)}) copy-start(bf16[8,384]{1,0:T(8,128)(2,1)} %get-tuple-element.5) | copy-start | bytes 18436
